TPU v7x, 256 devices: a whole 4x4x8 slice. The times are simulated.
256 devices in a mesh: ctx: 8 (over y, x_hi), head: 32 (over z, x_lo, core).
Axes of the slice: x: 4 (x_hi: 2, x_lo: 2; x = x_hi * 2 + x_lo), y: 4, z: 8, core: 2. Of those that a mesh axis runs over, the one named last changes fastest.
Arguments:
- queries: bfloat16 [2048, 128, 128], P('ctx', 'head'), may hold values from -24 to 24
- cache_keys: bfloat16 [8, 6144, 128], P(None, 'ctx'), may hold values from -12 to 12
- cache_values: bfloat16 [8, 6144, 128], P(None, 'ctx'), may hold values from -6 to 6
- scale_index: int32 [8, 48], P(None, 'ctx'), may hold values from 0 to 63
- scale_table: float32 [2, 64], replicated, may hold values from 0.6 to 1.6
- hist_lengths: int32 [8], P('ctx'), may hold values from 192 to 768, as said below
- span_offsets: int32 [16], replicated, may hold values from 0 to 6144
- new_keys: bfloat16 [2048, 8, 128], P('ctx'), may hold values from -12 to 12
- new_values: bfloat16 [2048, 8, 128], P('ctx'), may hold values from -6 to 6
- head_groups: int32 [128], P('head'), may hold values from 0 to 7, as said below
- out_weight: bfloat16 [16384, 8192], P('head'), may hold values from -0.75 to 0.75
Outputs:
- projected: bfloat16 [2048, 8192], P('ctx', 'head')
Inputs may be any that keep to these rules, and one draw needn't show every extreme that they name: `head_groups`: each key-value head serves exactly 16 query heads. `hist_lengths`: at least one block is full.
All inputs are finite; a program needn't handle non-finite values.
Results may differ from a plain program's by a relative error of at most 0.0058.
Values may be sent and summed in bfloat16 or wider, within the bound.
No kernel may reach another device: no remote copies, remote signals or barrier semaphores. Data moves between devices by JAX's collectives and lax.ppermute only.
A program may use at most 64 MiB of HBM per device.

v0:
```python
import math

import jax
import jax.numpy as jnp
from jax import lax
from jax.sharding import PartitionSpec as P

SPAN = 128


floor_score = -1e30


def entering(part, axis, combine, identity):
    place = lax.axis_index(axis)
    gathered = lax.all_gather(part, axis)
    state = jnp.zeros_like(part) + jnp.asarray(identity, part.dtype)

    def one(hop, state):
        return combine(state, lax.dynamic_index_in_dim(gathered, hop, 0, False))

    return lax.fori_loop(0, place, one, state)


def passed_along(value, axis, steps):
    count = lax.axis_size(axis)
    pairs = [(source, (source + steps) % count) for source in range(count)]
    return lax.ppermute(value, axis, pairs)


def add_counts(earlier, later):
    return earlier + later


def shards(
    queries,
    cache_keys,
    cache_values,
    scale_index,
    scale_table,
    hist_lengths,
    span_offsets,
    new_keys,
    new_values,
    head_groups,
    out_weight,
):
    ctx_count = lax.axis_size("ctx")
    position_me = lax.axis_index("ctx")
    row_count, heads_here, head_width = queries.shape
    slot_count = cache_keys.shape[1]
    spans_here = row_count // SPAN
    inverse = 1.0 / math.sqrt(head_width)
    codes = jnp.arange(scale_table.shape[1], dtype=jnp.int32)
    one_hot = (scale_index[:, :, None] == codes[None, None, :]).astype(jnp.float32)
    block_scales = jnp.einsum("kbn,tn->tkb", one_hot, scale_table, precision=lax.Precision.HIGHEST)
    slot_scales = jnp.repeat(block_scales, slot_count // scale_index.shape[1], axis=2)
    head_scales = jnp.take(slot_scales, head_groups, axis=1)
    per_block_key_scales = head_scales[0] * inverse
    value_scales = head_scales[1]
    keys_here = jnp.take(cache_keys, head_groups, axis=0)
    values_here = jnp.take(cache_values, head_groups, axis=0)
    start_slot = entering(hist_lengths, "ctx", add_counts, jnp.zeros_like(hist_lengths))
    slot_ids = jnp.arange(slot_count, dtype=jnp.int32)
    live = slot_ids < hist_lengths[0]
    positions = start_slot[0] + slot_ids

    def block_partial(query_block, source):
        offsets = lax.dynamic_slice_in_dim(span_offsets, source * spans_here, spans_here)
        limits = jnp.repeat(offsets, SPAN)
        visible = live[None, :] & (positions[None, :] < limits[:, None])
        unscaled_scores = jnp.einsum(
            "rhd,hsd->hrs", query_block, keys_here, preferred_element_type=jnp.float32
        )
        logit_scores = unscaled_scores * per_block_key_scales[:, None, :]
        masked = jnp.where(visible[None], logit_scores, floor_score)
        block_top = jnp.max(masked, axis=2)
        block_expo = jnp.where(visible[None], jnp.exp(masked - block_top[:, :, None]), 0.0)
        any_visible = jnp.any(visible, axis=1)
        block_total = jnp.where(any_visible[None, :], jnp.sum(block_expo, axis=2), 1.0)
        weights = (block_expo * value_scales[:, None, :]).astype(jnp.bfloat16)
        mixed = jnp.einsum("hrs,hsd->rhd", weights, values_here, preferred_element_type=jnp.float32)
        mixed = mixed / jnp.transpose(block_total)[:, :, None]
        block_lse = jnp.where(any_visible[None, :], block_top + jnp.log(block_total), floor_score)
        return (mixed.astype(jnp.bfloat16), block_lse)

    def record(parts, lses, source, query_block):
        part, block_lse = block_partial(query_block, source)
        parts = lax.dynamic_update_index_in_dim(parts, part, source, 0)
        lses = lax.dynamic_update_index_in_dim(lses, block_lse, source, 0)
        return (parts, lses)

    def forward(query_block):
        return passed_along(query_block, "ctx", 1)

    parts = jnp.zeros((ctx_count, row_count, heads_here, head_width), jnp.bfloat16)
    lses = jnp.full((ctx_count, heads_here, row_count), floor_score, jnp.float32)
    parts, lses = record(parts, lses, position_me, queries)

    def one_turn(turn, carry):
        travelling, parts_now, lses_now = carry
        travelling = forward(travelling)
        parts_now, lses_now = record(
            parts_now, lses_now, (position_me - turn) % ctx_count, travelling
        )
        return (travelling, parts_now, lses_now)

    travelling, parts, lses = lax.fori_loop(1, ctx_count, one_turn, (queries, parts, lses))
    query_spans = queries.reshape(spans_here, SPAN, heads_here, head_width)
    fresh_keys = jnp.take(new_keys, head_groups, axis=1).reshape(
        spans_here, SPAN, heads_here, head_width
    )
    fresh_values = jnp.take(new_values, head_groups, axis=1).reshape(
        spans_here, SPAN, heads_here, head_width
    )
    causal = jnp.arange(SPAN)[:, None] >= jnp.arange(SPAN)[None, :]
    fresh_raw = (
        jnp.einsum("crhd,cshd->chrs", query_spans, fresh_keys, preferred_element_type=jnp.float32)
        * inverse
    )
    fresh_masked = jnp.where(causal[None, None], fresh_raw, floor_score)
    fresh_top = jnp.max(fresh_masked, axis=3)
    fresh_expo = jnp.where(causal[None, None], jnp.exp(fresh_masked - fresh_top[..., None]), 0.0)
    fresh_total = jnp.sum(fresh_expo, axis=3)
    fresh_weights = fresh_expo.astype(jnp.bfloat16)
    fresh = jnp.einsum(
        "chrs,cshd->crhd", fresh_weights, fresh_values, preferred_element_type=jnp.float32
    )
    fresh = fresh / jnp.transpose(fresh_total, (0, 2, 1))[..., None]
    fresh = fresh.reshape(row_count, heads_here, head_width)
    fresh_lse = jnp.transpose(fresh_top + jnp.log(fresh_total), (1, 0, 2)).reshape(
        heads_here, row_count
    )
    home_parts, home_lses = (
        lax.all_to_all(parts.astype(jnp.float32), "ctx", split_axis=0, concat_axis=0, tiled=True),
        lax.all_to_all(lses, "ctx", split_axis=0, concat_axis=0, tiled=True),
    )
    peak = jnp.maximum(jnp.max(home_lses, axis=0), fresh_lse)
    block_weight = jnp.exp(home_lses - peak[None])
    fresh_weight = jnp.exp(fresh_lse - peak)
    numer_all = jnp.transpose(fresh_weight)[:, :, None] * fresh
    numer_all = numer_all + jnp.sum(
        jnp.transpose(block_weight, (0, 2, 1))[..., None] * home_parts, axis=0
    )
    denom_all = fresh_weight + jnp.sum(block_weight, axis=0)
    attended = (numer_all / jnp.transpose(denom_all)[:, :, None]).astype(jnp.bfloat16)
    flat = attended.reshape(row_count, heads_here * head_width)
    mine = lax.psum_scatter(
        lax.dot_general(
            out_weight, flat, (((0,), (1,)), ((), ())), preferred_element_type=jnp.float32
        ),
        "head",
        scatter_dimension=0,
        tiled=True,
    )
    return jnp.transpose(mine).astype(jnp.bfloat16)


def solution(mesh):
    placed = (
        P("ctx", "head", None),
        P(None, "ctx", None),
        P(None, "ctx", None),
        P(None, "ctx"),
        P(),
        P("ctx"),
        P(),
        P("ctx", None, None),
        P("ctx", None, None),
        P("head"),
        P("head", None),
    )
    return jax.shard_map(
        shards, mesh=mesh, in_specs=placed, out_specs=P("ctx", "head"), check_vma=False
    )
```

profile of v0, /device:TPU:8, one launch (start us, length us, event | category | flops | bytes accessed | tf_op | source)
XLA Modules:
  0.0 357.7 jit_solution(9188725824069449142)
XLA Ops:
  9.4 1.3 dynamic-slice
  11.4 12.0 %all-reduce = s32[8]{0:T(128)S(1)} all-reduce(s32[8]{0:T(128)S(1)} %dynamic-update-slice), channel_id=2, replica_groups=mesh['ctx'=8,'head'=32] {'ctx'}, use_global_device_ids=true, to_apply=%add | all-reduce | flops 8 | bytes 64
  23.4 2.3 while.30
  26.5 1.0 convolution_bitcast_fusion.2
  28.4 1.7 copy.66
  30.8 2.9 gather_fusion.2
  33.7 1.3 broadcast_select_fusion
  36.0 0.9 fusion.17
  37.0 2.5 fusion.26
  39.5 1.2 copy.65
  42.5 1.3 copy-done.1
  43.8 99.8 %while.31 = (s32[]{:T(128)}, bf16[256,4,128]{2,0,1:T(8,128)(2,1)S(1)}, bf16[8,256,4,128]{3,1,2,0:T(8,128)(2,1)}, f32[8,4,256]{2,1,0:T(4,128)}, s32[]{:T(128)}, /...) while((s32[]{:T(128)}, ...), condition=%wide.region_11.14_spmd.clone, body=%wide.region_7.13_spmd.clone.sunk | while | flops 414518528 | bytes 17140444 | solution.py:108
  43.8 4.2 %collective-permute-start = (bf16[256,4,128]{2,0,1:T(8,128)(2,1)S(1)}, bf16[256,4,128]{2,0,1:T(8,128)(2,1)S(1)}, u32[]{:S(2)}, u32[]{:S(2)}) collective-permute-start(bf16[256,4,128]{2,0,1:T(8,128)(2,1)S(1)} %get-tuple-element.599), channel_id=1, source_target_pairs={{0,32},{32,64},{64,96},{96,128},{128,160},{160,192},{192,224},{224... | collective-permute-start | bytes 786440 | tf_op jit(solution)/shard_map/while/body/eval_jaxpr/ppermute | solution.py:28
  49.1 3.5 collective-permute-done
  53.3 1.3 fusion.75
  55.2 2.1 bitcast_dynamic-update-slice_fusion.2
  57.3 3.4 collective-permute-start
  61.8 4.4 %collective-permute-done = bf16[256,4,128]{2,0,1:T(8,128)(2,1)S(1)} collective-permute-done((bf16[256,4,128]{2,0,1:T(8,128)(2,1)S(1)}, bf16[256,4,128]{2,0,1:T(8,128)(2,1)S(1)}, u32[]{:S(2)}, u32[]{:S(2)}) %collective-permute-start) | collective-permute-done | bytes 262176 | tf_op jit(solution)/shard_map/while/body/eval_jaxpr/ppermute | solution.py:28
  66.8 1.3 fusion.75
  68.7 2.0 bitcast_dynamic-update-slice_fusion.2
  70.8 2.5 collective-permute-start
  74.4 5.3 %collective-permute-done = bf16[256,4,128]{2,0,1:T(8,128)(2,1)S(1)} collective-permute-done((bf16[256,4,128]{2,0,1:T(8,128)(2,1)S(1)}, bf16[256,4,128]{2,0,1:T(8,128)(2,1)S(1)}, u32[]{:S(2)}, u32[]{:S(2)}) %collective-permute-start) | collective-permute-done | bytes 262176 | tf_op jit(solution)/shard_map/while/body/eval_jaxpr/ppermute | solution.py:28
  80.5 1.3 fusion.75
  82.3 2.1 bitcast_dynamic-update-slice_fusion.2
  84.4 1.5 collective-permute-start
  87.0 7.5 %collective-permute-done = bf16[256,4,128]{2,0,1:T(8,128)(2,1)S(1)} collective-permute-done((bf16[256,4,128]{2,0,1:T(8,128)(2,1)S(1)}, bf16[256,4,128]{2,0,1:T(8,128)(2,1)S(1)}, u32[]{:S(2)}, u32[]{:S(2)}) %collective-permute-start) | collective-permute-done | bytes 262176 | tf_op jit(solution)/shard_map/while/body/eval_jaxpr/ppermute | solution.py:28
  95.2 1.3 fusion.75
  97.1 2.1 bitcast_dynamic-update-slice_fusion.2
  100.4 8.8 %collective-permute-done = bf16[256,4,128]{2,0,1:T(8,128)(2,1)S(1)} collective-permute-done((bf16[256,4,128]{2,0,1:T(8,128)(2,1)S(1)}, bf16[256,4,128]{2,0,1:T(8,128)(2,1)S(1)}, u32[]{:S(2)}, u32[]{:S(2)}) %collective-permute-start) | collective-permute-done | bytes 262176 | tf_op jit(solution)/shard_map/while/body/eval_jaxpr/ppermute | solution.py:28
  110.0 1.3 fusion.75
  111.9 2.1 bitcast_dynamic-update-slice_fusion.2
  115.2 8.8 %collective-permute-done = bf16[256,4,128]{2,0,1:T(8,128)(2,1)S(1)} collective-permute-done((bf16[256,4,128]{2,0,1:T(8,128)(2,1)S(1)}, bf16[256,4,128]{2,0,1:T(8,128)(2,1)S(1)}, u32[]{:S(2)}, u32[]{:S(2)}) %collective-permute-start) | collective-permute-done | bytes 262176 | tf_op jit(solution)/shard_map/while/body/eval_jaxpr/ppermute | solution.py:28
  124.8 1.3 fusion.75
  126.7 2.1 bitcast_dynamic-update-slice_fusion.2
  130.0 8.9 %collective-permute-done = bf16[256,4,128]{2,0,1:T(8,128)(2,1)S(1)} collective-permute-done((bf16[256,4,128]{2,0,1:T(8,128)(2,1)S(1)}, bf16[256,4,128]{2,0,1:T(8,128)(2,1)S(1)}, u32[]{:S(2)}, u32[]{:S(2)}) %collective-permute-start) | collective-permute-done | bytes 262176 | tf_op jit(solution)/shard_map/while/body/eval_jaxpr/ppermute | solution.py:28
  139.6 1.3 fusion.75
  141.5 2.1 bitcast_dynamic-update-slice_fusion.2
  143.6 11.5 %all-to-all-start = ((f32[8,4,256]{2,1,0:T(4,128)}), f32[8,4,256]{2,1,0:T(4,128)S(1)}, u32[]{:S(2)}, u32[]{:S(2)}) async-start(f32[8,4,256]{2,1,0:T(4,128)} %get-tuple-element.319), calls=%async_computation | async-start | bytes 65536 | tf_op jit(solution)/shard_map/all_to_all | solution.py:136
  155.1 4.0 %convert_element_type.46 = f32[8,256,4,128]{3,1,2,0:T(8,128)} convert(bf16[8,256,4,128]{3,1,2,0:T(8,128)(2,1)} %get-tuple-element.320) | non-fusion elementwise | flops 1048576 | bytes 6291456 | tf_op jit(solution)/shard_map/convert_element_type | solution.py:135
  159.1 2.4 all-to-all-done
  161.5 9.1 %all-to-all-start.1 = ((f32[8,256,4,128]{3,1,2,0:T(8,128)}), f32[8,256,4,128]{3,1,2,0:T(8,128)}, u32[]{:S(2)}, u32[]{:S(2)}) async-start(f32[8,256,4,128]{3,1,2,0:T(8,128)} %convert_element_type.46), calls=%async_computation.1 | async-start | bytes 8388608 | tf_op jit(solution)/shard_map/all_to_all | solution.py:135
  170.7 1.7 gather_fusion.4
  172.5 1.7 gather_fusion.1
  175.9 29.8 %all-to-all-done.1 = f32[8,256,4,128]{3,1,2,0:T(8,128)} async-done(((f32[8,256,4,128]{3,1,2,0:T(8,128)}), f32[8,256,4,128]{3,1,2,0:T(8,128)}, u32[]{:S(2)}, u32[]{:S(2)}) %all-to-all-start.1) | async-done | bytes 4194336 | tf_op jit(solution)/shard_map/all_to_all | solution.py:135
  205.7 2.9 multiply_reduce_fusion
  209.6 9.0 %convolution_bitcast_fusion = f32[8192,256]{0,1:T(8,128)} fusion(bf16[512,8192]{1,0:T(8,128)(2,1)} %param.29, f32[32,8,4,128]{3,2,1,0:T(4,128)S(1)} %bitcast.175, f32[256,512]{1,0:T(8,128)S(1)} %copy.73, f32[32,8,4,128]{3,2,1,0:T(4,128)S(1)} %bitcast.177, f32[32,8,4,128]{3,2,1,0:T(4,128)S(1)} %bitcast.176), kind=kOutput, calls=%fused_computation.31 | convolution fusion | flops 2148007936 | bytes 18874368 | tf_op jit(solution)/shard_map/dot_general | solution.py:149
  218.7 130.6 %reduce-scatter.2.cloned.1.call-done = f32[256,256]{0,1:T(8,128)} async-done(((f32[8192,256]{0,1:T(8,128)}), f32[256,256]{0,1:T(8,128)}) %reduce-scatter.2.cloned.1.call-update) | async-done | bytes 262160 | tf_op jit(solution)/shard_map/reduce_scatter | solution.py:148
  349.3 1.6 convert_bitcast_fusion
  (141 shorter events, 29.3 us)
Async XLA Ops:
  6.5 23.6 %copy-start = (bf16[8,768,128]{2,1,0:T(8,128)(2,1)S(1)}, bf16[8,768,128]{2,1,0:T(8,128)(2,1)}, u32[]{:S(2)}) copy-start(bf16[8,768,128]{2,1,0:T(8,128)(2,1)} %param.20) | copy-start | bytes 4718596
  30.1 5.3 %copy-start.6 = (bf16[256,4,128]{2,1,0:T(4,128)(2,1)S(1)}, bf16[256,4,128]{2,1,0:T(4,128)(2,1)}, u32[]{:S(2)}) copy-start(bf16[256,4,128]{2,1,0:T(4,128)(2,1)} %param.19) | copy-start | bytes 786436
  35.1 1.9 copy-start.4
  39.5 4.3 %copy-start.7 = (bf16[256,4,128]{2,0,1:T(8,128)(2,1)S(1)}, bf16[256,4,128]{2,0,1:T(8,128)(2,1)}, u32[]{:S(2)}) copy-start(bf16[256,4,128]{2,0,1:T(8,128)(2,1)} %copy.66) | copy-start | bytes 786436
  39.5 4.3 %copy-start.8 = (s32[16]{0:T(128)S(1)}, s32[16]{0:T(128)}, u32[]{:S(2)}) copy-start(s32[16]{0:T(128)} %param.25) | copy-start | bytes 196
  42.5 1.3 copy-start.1
  43.8 8.8 %collective-permute-start = (bf16[256,4,128]{2,0,1:T(8,128)(2,1)S(1)}, bf16[256,4,128]{2,0,1:T(8,128)(2,1)S(1)}, u32[]{:S(2)}, u32[]{:S(2)}) collective-permute-start(bf16[256,4,128]{2,0,1:T(8,128)(2,1)S(1)} %get-tuple-element.599), channel_id=1, source_target_pairs={{0,32},{32,64},{64,96},{96,128},{128,160},{160,192},{192,224},{224... | collective-permute-start | bytes 786440 | tf_op jit(solution)/shard_map/while/body/eval_jaxpr/ppermute | solution.py:28
  52.6 2.6 copy-start.5
  57.3 8.9 %collective-permute-start = (bf16[256,4,128]{2,0,1:T(8,128)(2,1)S(1)}, bf16[256,4,128]{2,0,1:T(8,128)(2,1)S(1)}, u32[]{:S(2)}, u32[]{:S(2)}) collective-permute-start(bf16[256,4,128]{2,0,1:T(8,128)(2,1)S(1)} %get-tuple-element.599), channel_id=1, source_target_pairs={{0,32},{32,64},{64,96},{96,128},{128,160},{160,192},{192,224},{224... | collective-permute-start | bytes 786440 | tf_op jit(solution)/shard_map/while/body/eval_jaxpr/ppermute | solution.py:28
  66.1 2.6 copy-start.5
  70.8 8.9 %collective-permute-start = (bf16[256,4,128]{2,0,1:T(8,128)(2,1)S(1)}, bf16[256,4,128]{2,0,1:T(8,128)(2,1)S(1)}, u32[]{:S(2)}, u32[]{:S(2)}) collective-permute-start(bf16[256,4,128]{2,0,1:T(8,128)(2,1)S(1)} %get-tuple-element.599), channel_id=1, source_target_pairs={{0,32},{32,64},{64,96},{96,128},{128,160},{160,192},{192,224},{224... | collective-permute-start | bytes 786440 | tf_op jit(solution)/shard_map/while/body/eval_jaxpr/ppermute | solution.py:28
  79.7 2.6 copy-start.5
  84.4 10.1 %collective-permute-start = (bf16[256,4,128]{2,0,1:T(8,128)(2,1)S(1)}, bf16[256,4,128]{2,0,1:T(8,128)(2,1)S(1)}, u32[]{:S(2)}, u32[]{:S(2)}) collective-permute-start(bf16[256,4,128]{2,0,1:T(8,128)(2,1)S(1)} %get-tuple-element.599), channel_id=1, source_target_pairs={{0,32},{32,64},{64,96},{96,128},{128,160},{160,192},{192,224},{224... | collective-permute-start | bytes 786440 | tf_op jit(solution)/shard_map/while/body/eval_jaxpr/ppermute | solution.py:28
  94.5 2.6 copy-start.5
  99.2 10.1 %collective-permute-start = (bf16[256,4,128]{2,0,1:T(8,128)(2,1)S(1)}, bf16[256,4,128]{2,0,1:T(8,128)(2,1)S(1)}, u32[]{:S(2)}, u32[]{:S(2)}) collective-permute-start(bf16[256,4,128]{2,0,1:T(8,128)(2,1)S(1)} %get-tuple-element.599), channel_id=1, source_target_pairs={{0,32},{32,64},{64,96},{96,128},{128,160},{160,192},{192,224},{224... | collective-permute-start | bytes 786440 | tf_op jit(solution)/shard_map/while/body/eval_jaxpr/ppermute | solution.py:28
  109.3 2.6 copy-start.5
  114.0 10.0 %collective-permute-start = (bf16[256,4,128]{2,0,1:T(8,128)(2,1)S(1)}, bf16[256,4,128]{2,0,1:T(8,128)(2,1)S(1)}, u32[]{:S(2)}, u32[]{:S(2)}) collective-permute-start(bf16[256,4,128]{2,0,1:T(8,128)(2,1)S(1)} %get-tuple-element.599), channel_id=1, source_target_pairs={{0,32},{32,64},{64,96},{96,128},{128,160},{160,192},{192,224},{224... | collective-permute-start | bytes 786440 | tf_op jit(solution)/shard_map/while/body/eval_jaxpr/ppermute | solution.py:28
  124.1 2.6 copy-start.5
  128.8 10.1 %collective-permute-start = (bf16[256,4,128]{2,0,1:T(8,128)(2,1)S(1)}, bf16[256,4,128]{2,0,1:T(8,128)(2,1)S(1)}, u32[]{:S(2)}, u32[]{:S(2)}) collective-permute-start(bf16[256,4,128]{2,0,1:T(8,128)(2,1)S(1)} %get-tuple-element.599), channel_id=1, source_target_pairs={{0,32},{32,64},{64,96},{96,128},{128,160},{160,192},{192,224},{224... | collective-permute-start | bytes 786440 | tf_op jit(solution)/shard_map/while/body/eval_jaxpr/ppermute | solution.py:28
  138.9 2.6 copy-start.5
  143.6 18.0 %all-to-all-start = ((f32[8,4,256]{2,1,0:T(4,128)}), f32[8,4,256]{2,1,0:T(4,128)S(1)}, u32[]{:S(2)}, u32[]{:S(2)}) async-start(f32[8,4,256]{2,1,0:T(4,128)} %get-tuple-element.319), calls=%async_computation | async-start | bytes 65536 | tf_op jit(solution)/shard_map/all_to_all | solution.py:136
  159.1 11.6 %copy-start.2 = (bf16[256,8,128]{2,1,0:T(8,128)(2,1)S(1)}, bf16[256,8,128]{2,1,0:T(8,128)(2,1)}, u32[]{:S(2)}) copy-start(bf16[256,8,128]{2,1,0:T(8,128)(2,1)} %param.27) | copy-start | bytes 1572868
  161.5 44.1 %all-to-all-start.1 = ((f32[8,256,4,128]{3,1,2,0:T(8,128)}), f32[8,256,4,128]{3,1,2,0:T(8,128)}, u32[]{:S(2)}, u32[]{:S(2)}) async-start(f32[8,256,4,128]{3,1,2,0:T(8,128)} %convert_element_type.46), calls=%async_computation.1 | async-start | bytes 8388608 | tf_op jit(solution)/shard_map/all_to_all | solution.py:135
  170.7 1.8 copy-start.3
  170.7 178.6 %reduce-scatter.2.cloned.1.call-start = ((), (), s32[]{:S(2)}) async-start(), calls=%async_computation.3 | async-start | bytes 8650752 | tf_op jit(solution)/shard_map/reduce_scatter | solution.py:148
Sparse Core Ops, SparseCore 0:
  218.8 130.4 reduce-scatter.1
where the time goes:
time: 358 us
  waiting for transfers between devices  210 us (59%)
  other arithmetic  33.5 us (9%)
  matrix products  33.3 us (9%)
  starting transfers between devices  32.4 us (9%)
  local copies, waits for them, and re-layouts  20.6 us (6%)
  between operations  14.3 us (4%)
  blocking collectives  12 us (3%)
    reduce_scatter x1, waiting for transfers between devices, shards(): lax.psum_scatter(lax.dot_general(out_weight, flat, (((0,), (1,)), ((), ()...  131 us
    ppermute x7, waiting for transfers between devices, passed_along(): return lax.ppermute(value, axis, pairs)  47.1 us
    all_to_all x1, waiting for transfers between devices, shards(): lax.all_to_all(parts.astype(jnp.float32), 'ctx', split_axis=0, concat_axi...  29.8 us
    dot_general x8, matrix products, block_partial(): jnp.einsum('hrs,hsd->rhd', weights, values_here, preferred_element_type=j...  17 us
    unnamed x1, blocking collectives  12 us
    ppermute x7, starting transfers between devices, passed_along(): return lax.ppermute(value, axis, pairs)  11.8 us
    all_to_all x1, starting transfers between devices, shards(): lax.all_to_all(lses, 'ctx', split_axis=0, concat_axis=0, tiled=True)  11.5 us
    reduce_sum x8, other arithmetic, block_partial(): jnp.sum(block_expo, axis=2)  9.75 us
  transfers between devices with their start and end apart: 10, of which 10 were waited for; matrix products, arithmetic and copies ran while one was open for 5% of the time, Pallas kernels for 0%

commit v1 on v0

v1 whole, which is shorter than its diff:
```python
import functools
import math

import jax
import jax.numpy as jnp
from jax import lax
from jax.experimental import pallas as pl
from jax.experimental.pallas import tpu as pltpu
from jax.sharding import PartitionSpec as P

SPAN = 128
SBLK = 128
HEADS = 4
ROWS = 256
DH = 128
SLOTS = 768
BLOCKS = SLOTS // SBLK
PART_ROWS = HEADS * DH
LSE_ROWS = 32
MSG_ROWS = PART_ROWS + LSE_ROWS
FLOOR = -1e30
LOG2E = math.log2(math.e)
INVERSE = 1.0 / math.sqrt(DH)
AXES = ("ctx", "head")
F32, BF16, I32 = jnp.float32, jnp.bfloat16, jnp.int32
VMEM_LIMIT = 24 * 1024 * 1024
HPS = 2


def linear(y, xh, z, xl, core):
    return (((y % 4) * 2 + xh % 2) * 8 + z % 8) * 4 + (xl % 2) * 2 + core % 2


def moved(dy=0, dxh=0, dz=0, dxl=0, dcore=0):
    return [
        (linear(y, xh, z, xl, c), linear(y + dy, xh + dxh, z + dz, xl + dxl, c + dcore))
        for y in range(4)
        for xh in range(2)
        for z in range(8)
        for xl in range(2)
        for c in range(2)
    ]


def send(value, **move):
    return lax.ppermute(value, AXES, moved(**move))


def params():
    return pltpu.CompilerParams(vmem_limit_bytes=VMEM_LIMIT)


def log2(value):
    return jnp.log(value) * LOG2E


def pack_lse(lse8):
    high = lse8.astype(BF16).astype(F32)
    rest = lse8 - high
    middle = rest.astype(BF16).astype(F32)
    low = (rest - middle).astype(BF16).astype(F32)
    return jnp.concatenate([high, middle, low, jnp.zeros_like(low)], axis=0).astype(BF16)


def unpack_lse(packed):
    wide = packed.astype(F32)
    return wide[0:8] + wide[8:16] + wide[16:24]


def history_kernel(merge, groups, counts, scale_index, scale_table, *refs):
    q_ref = refs[0]
    k_refs = refs[1 : 1 + HPS]
    v_refs = refs[1 + HPS : 1 + 2 * HPS]
    rest = refs[1 + 2 * HPS :]
    if merge:
        prev_ref, prev_lse_ref, out_ref, lse_ref, weights_ref, held_ref = rest
    else:
        out_ref, lse_ref, weights_ref = rest
    step = pl.program_id(0)

    @pl.when(step == 0)
    def _():
        lse_ref[...] = jnp.full((8, ROWS), FLOOR, F32)
        if merge:
            held_ref[...] = unpack_lse(prev_lse_ref[...])

    lane = lax.broadcasted_iota(I32, (1, ROWS), 1)
    count = jnp.where(lane < SPAN, counts[0], counts[1])
    slot = lax.broadcasted_iota(I32, (SBLK, ROWS), 0)
    for local in range(HPS):
        head = step * HPS + local
        group = groups[head]
        query = q_ref[pl.ds(local * ROWS, ROWS), :]
        raw = lax.dot_general(
            k_refs[local][0], query, (((1,), (1,)), ((), ())), preferred_element_type=F32
        )
        scores = []
        for block in range(BLOCKS):
            scale = scale_table[0, scale_index[group, block]] * (INVERSE * LOG2E)
            piece = raw[block * SBLK : (block + 1) * SBLK] * scale
            scores.append(jnp.where(slot < count - block * SBLK, piece, FLOOR))
        top = functools.reduce(jnp.maximum, scores)
        top = jnp.max(top, axis=0, keepdims=True)
        total = jnp.zeros((SBLK, ROWS), F32)
        for block in range(BLOCKS):
            scale = scale_table[1, scale_index[group, block]]
            expo = jnp.exp2(scores[block] - top)
            total = total + expo
            weights_ref[local, block * SBLK : (block + 1) * SBLK, :] = (expo * scale).astype(BF16)
        total = jnp.sum(total, axis=0, keepdims=True)
        mixed = jnp.dot(v_refs[local][0], weights_ref[local], preferred_element_type=F32)
        seen = count > 0
        lse = jnp.where(seen, top + log2(total), FLOOR)
        share = jnp.where(seen, 1.0 / total, 0.0)
        rows = pl.ds(local * DH, DH)
        if merge:
            before = held_ref[pl.ds(head, 1), :]
            peak = jnp.maximum(lse, before)
            mine = jnp.exp2(lse - peak)
            other = jnp.exp2(before - peak)
            both = mine + other
            inverse = 1.0 / both
            mixed = mixed * (share * mine * inverse)
            mixed = mixed + prev_ref[rows, :].astype(F32) * (other * inverse)
            lse = peak + log2(both)
        else:
            mixed = mixed * share
        out_ref[pl.ds(pl.multiple_of(head * DH, DH), DH), :] = mixed.astype(BF16)
        lse_ref[pl.ds(head, 1), :] = lse

    @pl.when(step == HEADS // HPS - 1)
    def _():
        out_ref[PART_ROWS:, :] = pack_lse(lse_ref[...])


def history(groups, counts, scale_index, scale_table, query, keys, values_t, previous=None):
    merge = previous is not None

    def of_group(local):
        return lambda i, g, *_: (g[i * HPS + local], 0, 0)

    in_specs = [pl.BlockSpec((HPS * ROWS, DH), lambda i, *_: (i, 0))]
    in_specs += [pl.BlockSpec((1, SLOTS, DH), of_group(local)) for local in range(HPS)]
    in_specs += [pl.BlockSpec((1, DH, SLOTS), of_group(local)) for local in range(HPS)]
    operands = [query] + [keys] * HPS + [values_t] * HPS
    scratch = [pltpu.VMEM((8, ROWS), F32), pltpu.VMEM((HPS, SLOTS, ROWS), BF16)]
    if merge:
        in_specs += [
            pl.BlockSpec((HPS * DH, ROWS), lambda i, *_: (i, 0)),
            pl.BlockSpec((LSE_ROWS, ROWS), lambda i, *_: (PART_ROWS // LSE_ROWS, 0)),
        ]
        operands += [previous, previous]
        scratch += [pltpu.VMEM((8, ROWS), F32)]
    return pl.pallas_call(
        functools.partial(history_kernel, merge),
        out_shape=jax.ShapeDtypeStruct((MSG_ROWS, ROWS), BF16),
        grid_spec=pltpu.PrefetchScalarGridSpec(
            num_scalar_prefetch=4,
            grid=(HEADS // HPS,),
            in_specs=in_specs,
            out_specs=pl.BlockSpec((MSG_ROWS, ROWS), lambda i, *_: (0, 0)),
            scratch_shapes=scratch,
        ),
        compiler_params=params(),
        cost_estimate=pl.CostEstimate(
            flops=4 * HEADS * ROWS * SLOTS * DH,
            bytes_accessed=2 * HEADS * SLOTS * DH * 2,
            transcendentals=HEADS * ROWS * SLOTS,
        ),
    )(groups, counts, scale_index, scale_table, *operands)


def fresh_kernel(groups, q_ref, k_ref, v_ref, out_ref, lse_ref):
    head = pl.program_id(0)

    @pl.when(head == 0)
    def _():
        lse_ref[...] = jnp.zeros((8, ROWS), F32)

    raw = lax.dot_general(
        k_ref[0], q_ref[...], (((1,), (1,)), ((), ())), preferred_element_type=F32
    )
    column = lax.broadcasted_iota(I32, (ROWS, ROWS), 0)
    row = lax.broadcasted_iota(I32, (ROWS, ROWS), 1)
    visible = (column <= row) & ((column >= SPAN) | (row < SPAN))
    score = jnp.where(visible, raw * (INVERSE * LOG2E), FLOOR)
    top = jnp.max(score, axis=0, keepdims=True)
    expo = jnp.exp2(score - top)
    total = jnp.sum(expo, axis=0, keepdims=True)
    mixed = jnp.dot(v_ref[0], expo.astype(BF16), preferred_element_type=F32)
    out_ref[...] = mixed * (1.0 / total)
    lse_ref[pl.ds(head, 1), :] = top + log2(total)


def fresh_part(groups, query, new_keys, new_values_t):
    return pl.pallas_call(
        fresh_kernel,
        out_shape=(
            jax.ShapeDtypeStruct((PART_ROWS, ROWS), F32),
            jax.ShapeDtypeStruct((8, ROWS), F32),
        ),
        grid_spec=pltpu.PrefetchScalarGridSpec(
            num_scalar_prefetch=1,
            grid=(HEADS,),
            in_specs=[
                pl.BlockSpec((ROWS, DH), lambda i, *_: (i, 0)),
                pl.BlockSpec((1, ROWS, DH), lambda i, g: (g[i], 0, 0)),
                pl.BlockSpec((1, DH, ROWS), lambda i, g: (g[i], 0, 0)),
            ],
            out_specs=(
                pl.BlockSpec((DH, ROWS), lambda i, *_: (i, 0)),
                pl.BlockSpec((8, ROWS), lambda i, *_: (0, 0)),
            ),
        ),
        compiler_params=params(),
        cost_estimate=pl.CostEstimate(
            flops=4 * HEADS * ROWS * ROWS * DH,
            bytes_accessed=HEADS * ROWS * DH * 6,
            transcendentals=HEADS * ROWS * ROWS,
        ),
    )(groups, query, new_keys, new_values_t)


def combine_kernel(a_ref, b_ref, c_ref, d_ref, fresh_ref, fresh_lse_ref, out_ref):
    parts = (a_ref, b_ref, c_ref, d_ref)
    lses = [unpack_lse(part[PART_ROWS:, :]) for part in parts]
    fresh_lse = fresh_lse_ref[...]
    peak = functools.reduce(jnp.maximum, lses, fresh_lse)
    weights = [jnp.exp2(lse - peak) for lse in lses]
    fresh_weight = jnp.exp2(fresh_lse - peak)
    inverse = 1.0 / functools.reduce(jnp.add, weights, fresh_weight)
    weights = [weight * inverse for weight in weights]
    fresh_weight = fresh_weight * inverse
    for head in range(HEADS):
        rows = slice(head * DH, (head + 1) * DH)
        total = fresh_ref[rows, :] * fresh_weight[head : head + 1]
        for part, weight in zip(parts, weights):
            total = total + part[rows, :].astype(F32) * weight[head : head + 1]
        out_ref[:, rows] = jnp.transpose(total).astype(BF16)


def combined(parts, fresh, fresh_lse):
    return pl.pallas_call(
        combine_kernel,
        out_shape=jax.ShapeDtypeStruct((ROWS, PART_ROWS), BF16),
        in_specs=[pl.BlockSpec(memory_space=pltpu.VMEM)] * 6,
        out_specs=pl.BlockSpec(memory_space=pltpu.VMEM),
        compiler_params=params(),
        cost_estimate=pl.CostEstimate(
            flops=10 * ROWS * PART_ROWS, bytes_accessed=3 * 2**20, transcendentals=0
        ),
    )(*parts, fresh, fresh_lse)


def copy_kernel(core, w_ref, out_ref):
    out_ref[0] = w_ref[...]


def columns_of(core, weight):
    depth, width = weight.shape
    count = width // (2 * ROWS)
    return pl.pallas_call(
        copy_kernel,
        out_shape=jax.ShapeDtypeStruct((count, depth, ROWS), BF16),
        grid_spec=pltpu.PrefetchScalarGridSpec(
            num_scalar_prefetch=1,
            grid=(count,),
            in_specs=[pl.BlockSpec((depth, ROWS), lambda i, c: (0, 2 * i + c[0]))],
            out_specs=pl.BlockSpec((1, depth, ROWS), lambda i, c: (i, 0, 0)),
        ),
        compiler_params=params(),
        cost_estimate=pl.CostEstimate(
            flops=0, bytes_accessed=2 * depth * width, transcendentals=0
        ),
    )(core, weight)


def project_kernel(own_at, other_at, a_ref, b_ref, w_ref, v_ref, out_ref):
    total = jnp.dot(a_ref[...], w_ref[...], preferred_element_type=F32)
    total = total + jnp.dot(b_ref[...], v_ref[0], preferred_element_type=F32)
    out_ref[0] = total.astype(out_ref.dtype)


def projected(own_at, other_at, mine, theirs, weight, other_weight, kind):
    count = own_at.shape[0]
    depth = weight.shape[0]
    return pl.pallas_call(
        project_kernel,
        out_shape=jax.ShapeDtypeStruct((count, ROWS, ROWS), kind),
        grid_spec=pltpu.PrefetchScalarGridSpec(
            num_scalar_prefetch=2,
            grid=(count,),
            in_specs=[
                pl.BlockSpec((ROWS, depth), lambda i, *_: (0, 0)),
                pl.BlockSpec((ROWS, depth), lambda i, *_: (0, 0)),
                pl.BlockSpec((depth, ROWS), lambda i, a, b: (0, a[i])),
                pl.BlockSpec((1, depth, ROWS), lambda i, a, b: (b[i], 0, 0)),
            ],
            out_specs=pl.BlockSpec((1, ROWS, ROWS), lambda i, *_: (i, 0, 0)),
        ),
        compiler_params=params(),
        cost_estimate=pl.CostEstimate(
            flops=count * 4 * ROWS * ROWS * depth,
            bytes_accessed=count * 4 * ROWS * depth,
            transcendentals=0,
        ),
    )(own_at, other_at, mine, theirs, weight, other_weight)


def shards(
    queries,
    cache_keys,
    cache_values,
    scale_index,
    scale_table,
    hist_lengths,
    span_offsets,
    new_keys,
    new_values,
    head_groups,
    out_weight,
):
    ctx, place = lax.axis_index("ctx"), lax.axis_index("head")
    y, xh = ctx // 2, ctx % 2
    z, xl, core = place // 4, (place // 2) % 2, place % 2

    q0 = jnp.transpose(queries, (1, 0, 2)).reshape(HEADS * ROWS, DH)
    p0 = send(q0, dxh=1, dxl=1)
    q_down = send(q0, dy=1)
    q_up = send(q0, dy=-1)

    small = jnp.concatenate([head_groups, hist_lengths])
    small_pair = send(small, dxh=1, dxl=1)
    pair_groups = small_pair[:HEADS]
    pair_length = small_pair[HEADS:]
    both = hist_lengths + pair_length
    start = jnp.where(xh == 1, pair_length, 0)
    for step in (1, -1, 2):
        start = start + jnp.where((y - step) % 4 < y, send(both, dy=step), 0)
    start = start[0]
    length = hist_lengths[0]

    def counts(source_y, source_xh):
        source = (source_y % 4) * 2 + source_xh
        offsets = lax.dynamic_slice_in_dim(span_offsets, source * 2, 2)
        return jnp.clip(jnp.minimum(length, offsets - start), 0, SLOTS)

    q_far = send(q0, dy=2)
    p_down = send(p0, dy=1)
    p_up = send(p0, dy=-1)
    p_far = send(q_far, dxh=1, dxl=1)

    other_weight = send(columns_of((1 - core)[None], out_weight), dcore=1)
    values_t = jnp.swapaxes(cache_values, 1, 2)
    fresh, fresh_lse = fresh_part(
        head_groups,
        q0,
        jnp.transpose(new_keys, (1, 0, 2)),
        jnp.transpose(new_values, (1, 2, 0)),
    )

    def attend(groups, source_y, source_xh, query, previous=None):
        return history(
            groups,
            counts(source_y, source_xh),
            scale_index,
            scale_table,
            query,
            cache_keys,
            values_t,
            previous,
        )

    back = {}
    for step, query in ((0, p0), (-1, p_down), (1, p_up), (2, p_far)):
        back[step] = send(attend(pair_groups, y + step, 1 - xh, query), dxh=1, dxl=1)
    parts = []
    for step, query in ((0, q0), (-1, q_down), (1, q_up), (2, q_far)):
        part = attend(head_groups, y + step, xh, query, back[step])
        parts.append(send(part, dy=step) if step else part)

    mine = combined(parts, fresh, fresh_lse)
    theirs = send(mine, dcore=1)

    def project(steps, kind=F32):
        at = jnp.stack([((z + step) % 8) * 2 + xl ^ other for step, other in steps])
        return projected(2 * at + core, at, mine, theirs, out_weight, other_weight, kind)

    first = project([(4, 0), (4, 1)], BF16)
    up = send(first[0:1], dz=1)
    down = send(first[1:2], dz=-1)
    for step in (3, 2, 1):
        partial = project([(step, 0), (step, 1), (-step, 0), (-step, 1)])
        if step == 3:
            up = jnp.concatenate([partial[0:1] + up.astype(F32), partial[1:2]])
            down = jnp.concatenate([partial[2:3], partial[3:4] + down.astype(F32)])
        else:
            up = partial[0:2] + up.astype(F32)
            down = partial[2:4] + down.astype(F32)
        up = send(up.astype(BF16), dz=1)
        down = send(down.astype(BF16), dz=-1)
    partial = project([(0, 0), (0, 1)])
    total = partial + up.astype(F32) + down.astype(F32)
    across = send(total[1].astype(BF16), dxl=1)
    return (total[0] + across.astype(F32)).astype(BF16)


def solution(mesh):
    placed = (
        P("ctx", "head", None),
        P(None, "ctx", None),
        P(None, "ctx", None),
        P(None, "ctx"),
        P(),
        P("ctx"),
        P(),
        P("ctx", None, None),
        P("ctx", None, None),
        P("head"),
        P("head", None),
    )
    return jax.shard_map(
        shards, mesh=mesh, in_specs=placed, out_specs=P("ctx", "head"), check_vma=False
    )
```

time: 358 us -> 166 us (0.46)
  waiting for transfers between devices: 210 us -> 31.4 us
  Pallas kernels: 0 us -> 59.8 us
  matrix products: 33.3 us -> 0 us
  other arithmetic: 33.5 us -> 1.66 us
  starting transfers between devices: 32.4 us -> 50.5 us
  blocking collectives: 12 us -> 0 us
  between operations: 14.3 us -> 4.08 us
    reduce_scatter x1 -> x0, waiting for transfers between devices: 131 us -> none  [shards(): lax.psum_scatter(lax.dot_general(out_weight, flat, (((0,), (1,)), ((), ()...]
    pallas_call x0 -> x16, Pallas kernels: none -> 59.8 us  [the longest x8 34.6 us: history(): pl.pallas_call(functools.partial(history_kernel, merge), out_shape=jax.Sh...]
    ppermute x7 -> x29, starting transfers between devices: 11.8 us -> 50.5 us  [send(): return lax.ppermute(value, AXES, moved(**move))]
    dot_general x20 -> x0, matrix products: 33.3 us -> none  [the longest x8 17 us: block_partial(): jnp.einsum('hrs,hsd->rhd', weights, values_here, preferred_element_type=j...]
    all_to_all x2 -> x0, waiting for transfers between devices: 32.2 us -> none  [the longest x1 29.8 us: shards(): lax.all_to_all(parts.astype(jnp.float32), 'ctx', split_axis=0, concat_axi...]
    all_to_all x2 -> x0, starting transfers between devices: 20.7 us -> none  [the longest x1 11.5 us: shards(): lax.all_to_all(lses, 'ctx', split_axis=0, concat_axis=0, tiled=True)]
    ppermute x7 -> x29, waiting for transfers between devices: 47.1 us -> 31.4 us  [send(): return lax.ppermute(value, AXES, moved(**move))]
    reduce_sum x10 -> x0, other arithmetic: 12.7 us -> none  [the longest x8 9.75 us: block_partial(): jnp.sum(block_expo, axis=2)]
  transfers between devices with their start and end apart: 10 -> 29, of which waited for: 10 -> 10; matrix products, arithmetic and copies ran while one was open for 5% -> 3% of each run, Pallas kernels for 0% -> 29%
where the time goes in v1:
time: 166 us; the launch traced here: 165 us
  Pallas kernels  59.8 us (36%)
  starting transfers between devices  50.5 us (30%)
  waiting for transfers between devices  31.4 us (19%)
  local copies, waits for them, and re-layouts  17.6 us (11%)
  between operations  4.08 us (2%)
    ppermute x29, starting transfers between devices, send(): return lax.ppermute(value, AXES, moved(**move))  50.5 us
    pallas_call x8, Pallas kernels, history(): pl.pallas_call(functools.partial(history_kernel, merge), out_shape=jax.Sh...  34.6 us
    ppermute x29, waiting for transfers between devices, send(): return lax.ppermute(value, AXES, moved(**move))  31.4 us
    unnamed x27, local copies, waits for them, and re-layouts  17 us
    pallas_call x5, Pallas kernels, projected(): pl.pallas_call(project_kernel, out_shape=jax.ShapeDtypeStruct((count, ROW...  15.1 us
    pallas_call x1, Pallas kernels, columns_of(): pl.pallas_call(copy_kernel, out_shape=jax.ShapeDtypeStruct((count, depth,...  6.35 us
  transfers between devices with their start and end apart: 29, of which 10 were waited for; matrix products, arithmetic and copies ran while one was open for 3% of the time, Pallas kernels for 29%

profile of v1, /device:TPU:8, one launch (start us, length us, event | category | flops | bytes accessed | tf_op | source)
XLA Modules:
  0.0 165.1 jit_solution(12825854499427534978)
XLA Ops:
  0.0 3.4 %copy-done.1 = bf16[512,8192]{1,0:T(8,128)(2,1)S(1)} copy-done((bf16[512,8192]{1,0:T(8,128)(2,1)S(1)}, bf16[512,8192]{1,0:T(8,128)(2,1)}, u32[]{:S(2)}) %copy-start.1) | copy-done | bytes 8388632
  3.4 6.3 %shard_map.119 = bf16[16,512,256]{2,1,0:T(8,128)(2,1)} custom-call(s32[1]{0:T(128)} %bitcast.13.core, bf16[512,8192]{1,0:T(8,128)(2,1)S(1)} %copy-done.1), custom_call_target="tpu_custom_call" | custom-call | bytes 8388608 | tf_op jit(solution)/shard_map/pallas_call | solution.py:262
  9.8 2.8 %collective-permute-start.4 = (bf16[1024,128]{1,0:T(8,128)(2,1)S(1)}, bf16[1024,128]{1,0:T(8,128)(2,1)}, u32[]{:S(2)}, u32[]{:S(2)}) collective-permute-start(bf16[1024,128]{1,0:T(8,128)(2,1)S(1)} %bitcast.56), channel_id=1, source_target_pairs={{0,34},{1,35},{2,32},{3,33},{4,38},{5,39},{6,36},{7,37},{8,42},{9,... | collective-permute-start | bytes 786440 | tf_op jit(solution)/shard_map/ppermute | solution.py:46
  12.7 2.3 %collective-permute-start.14 = (bf16[1024,128]{1,0:T(8,128)(2,1)S(1)}, bf16[1024,128]{1,0:T(8,128)(2,1)}, u32[]{:S(2)}, u32[]{:S(2)}) collective-permute-start(bf16[1024,128]{1,0:T(8,128)(2,1)S(1)} %bitcast.57), channel_id=1, source_target_pairs={{0,128},{1,129},{2,130},{3,131},{4,132},{5,133},{6,134},{7,135},{8... | collective-permute-start | bytes 786440 | tf_op jit(solution)/shard_map/ppermute | solution.py:46
  15.0 5.0 %collective-permute-done.4.refs_0_ = bf16[1024,128]{1,0:T(8,128)(2,1)} collective-permute-done((bf16[1024,128]{1,0:T(8,128)(2,1)S(1)}, bf16[1024,128]{1,0:T(8,128)(2,1)}, u32[]{:S(2)}, u32[]{:S(2)}) %collective-permute-start.4) | collective-permute-done | bytes 262176 | tf_op jit(solution)/shard_map/ppermute | solution.py:46
  19.9 1.6 collective-permute-start.7
  22.8 2.6 %collective-permute-start.15 = (bf16[1024,128]{1,0:T(8,128)(2,1)}, bf16[1024,128]{1,0:T(8,128)(2,1)}, u32[]{:S(2)}, u32[]{:S(2)}) collective-permute-start(bf16[1024,128]{1,0:T(8,128)(2,1)} %collective-permute-done.14.refs_0_), channel_id=1, source_target_pairs={{0,34},{1,35},{2,32},{3,33},{4,38},{5,39},{6,36},{7,37},{8,42},{9,... | collective-permute-start | bytes 786440 | tf_op jit(solution)/shard_map/ppermute | solution.py:46
  26.2 5.8 %collective-permute-done = s32[5]{0:T(128)S(1)} collective-permute-done((s32[5]{0:T(128)S(1)}, s32[5]{0:T(128)S(1)}, u32[]{:S(2)}, u32[]{:S(2)}) %collective-permute-start) | collective-permute-done | bytes 52 | tf_op jit(solution)/shard_map/ppermute | solution.py:46
  33.1 2.8 %collective-permute-start.1 = (s32[1]{0:T(128)}, s32[1]{0:T(128)}, u32[]{:S(2)}, u32[]{:S(2)}) collective-permute-start(s32[1]{0:T(128)} %add.259), channel_id=1, source_target_pairs={{0,64},{1,65},{2,66},{3,67},{4,68},{5,69},{6,70},{7,71},{8,72},{9,... | collective-permute-start | bytes 20 | tf_op jit(solution)/shard_map/ppermute | solution.py:46
  35.9 1.9 %collective-permute-done.1 = s32[1]{0:T(128)} collective-permute-done((s32[1]{0:T(128)}, s32[1]{0:T(128)}, u32[]{:S(2)}, u32[]{:S(2)}) %collective-permute-start.1) | collective-permute-done | bytes 36 | tf_op jit(solution)/shard_map/ppermute | solution.py:46
  37.8 4.5 %collective-permute-start.2 = (s32[1]{0:T(128)}, s32[1]{0:T(128)}, u32[]{:S(2)}, u32[]{:S(2)}) collective-permute-start(s32[1]{0:T(128)} %add.259), channel_id=1, source_target_pairs={{0,192},{1,193},{2,194},{3,195},{4,196},{5,197},{6,198},{7,199},{8... | collective-permute-start | bytes 20 | tf_op jit(solution)/shard_map/ppermute | solution.py:46
  42.3 3.7 %collective-permute-start.3 = (s32[1]{0:T(128)}, s32[1]{0:T(128)}, u32[]{:S(2)}, u32[]{:S(2)}) collective-permute-start(s32[1]{0:T(128)} %add.259), channel_id=1, source_target_pairs={{0,128},{1,129},{2,130},{3,131},{4,132},{5,133},{6,134},{7,135},{8... | collective-permute-start | bytes 20 | tf_op jit(solution)/shard_map/ppermute | solution.py:46
  46.0 1.5 collective-permute-done.3
  47.8 1.7 %copy.13 = bf16[8,768,128]{1,2,0:T(8,128)(2,1)S(1)} copy(bf16[8,768,128]{2,1,0:T(8,128)(2,1)} %param.13) | data formatting | bytes 3145728 | tf_op args[2]
  52.1 4.1 %shard_map.111 = bf16[544,256]{1,0:T(8,128)(2,1)S(1)} custom-call(s32[4]{0:T(128)S(1)} %bitcast.64, s32[2]{0:T(128)S(1)} %get-tuple-element.32.counts, s32[8,6]{1,0:T(8,128)S(1)} %copy-done.6, f32[2,64]{1,0:T(2,128)S(1)} %copy-done.7, bf16[1024,128]{1,0:T(8,128)(2,1)} %collective-permute-done.7.refs_0_, bf16[8,768,128]{2,1,0:T(8,128)(2,1)S(1)} %copy-done, ...), custom_call_target="tpu_custom_call" | custom-call | flops 402653184 | bytes 1572864 | tf_op jit(solution)/shard_map/pallas_call | solution.py:154
  56.1 1.9 %collective-permute-start.8 = (bf16[544,256]{1,0:T(8,128)(2,1)S(1)}, bf16[544,256]{1,0:T(8,128)(2,1)S(1)}, u32[]{:S(2)}, u32[]{:S(2)}) collective-permute-start(bf16[544,256]{1,0:T(8,128)(2,1)S(1)} %shard_map.111), channel_id=1, source_target_pairs={{0,34},{1,35},{2,32},{3,33},{4,38},{5,39},{6,36},{7,37},{8,42},{9,... | collective-permute-start | bytes 835592 | tf_op jit(solution)/shard_map/ppermute | solution.py:46
  58.1 1.4 collective-permute-start.10
  59.4 4.1 %shard_map.113 = bf16[544,256]{1,0:T(8,128)(2,1)S(1)} custom-call(s32[4]{0:T(128)S(1)} %bitcast.65, s32[2]{0:T(128)S(1)} %get-tuple-element.30.counts, s32[8,6]{1,0:T(8,128)S(1)} %copy-done.6, f32[2,64]{1,0:T(2,128)S(1)} %copy-done.7, bf16[1024,128]{1,0:T(8,128)(2,1)} %collective-permute-done.11.refs_0_, bf16[8,768,128]{2,1,0:T(8,128)(2,1)S(1)} %copy-done, ...), custom_call_target="tpu_custom_call" | custom-call | flops 402653184 | bytes 1572864 | tf_op jit(solution)/shard_map/pallas_call | solution.py:154
  63.5 2.4 %collective-permute-start.12 = (bf16[544,256]{1,0:T(8,128)(2,1)S(1)}, bf16[544,256]{1,0:T(8,128)(2,1)S(1)}, u32[]{:S(2)}, u32[]{:S(2)}) collective-permute-start(bf16[544,256]{1,0:T(8,128)(2,1)S(1)} %shard_map.113), channel_id=1, source_target_pairs={{0,34},{1,35},{2,32},{3,33},{4,38},{5,39},{6,36},{7,37},{8,42},{9,... | collective-permute-start | bytes 835592 | tf_op jit(solution)/shard_map/ppermute | solution.py:46
  66.0 4.1 %shard_map.115 = bf16[544,256]{1,0:T(8,128)(2,1)S(1)} custom-call(s32[4]{0:T(128)S(1)} %bitcast.66, s32[2]{0:T(128)S(1)} %get-tuple-element.29.counts, s32[8,6]{1,0:T(8,128)S(1)} %copy-done.6, f32[2,64]{1,0:T(2,128)S(1)} %copy-done.7, bf16[1024,128]{1,0:T(8,128)(2,1)} %collective-permute-done.15.refs_0_, bf16[8,768,128]{2,1,0:T(8,128)(2,1)S(1)} %copy-done, ...), custom_call_target="tpu_custom_call" | custom-call | flops 402653184 | bytes 1572864 | tf_op jit(solution)/shard_map/pallas_call | solution.py:154
  71.2 4.8 %shard_map.109 = bf16[544,256]{1,0:T(8,128)(2,1)} custom-call(s32[4]{0:T(128)S(1)} %bitcast.67, s32[2]{0:T(128)S(1)} %get-tuple-element.34.counts, s32[8,6]{1,0:T(8,128)S(1)} %copy-done.6, f32[2,64]{1,0:T(2,128)S(1)} %copy-done.7, bf16[1024,128]{1,0:T(8,128)(2,1)} %collective-permute-done.4.refs_0_, bf16[8,768,128]{2,1,0:T(8,128)(2,1)S(1)} %copy-done, ...), custom_call_target="tpu_custom_call" | custom-call | flops 402653184 | bytes 1572864 | tf_op jit(solution)/shard_map/pallas_call | solution.py:154
  76.0 2.1 %collective-permute-start.5 = (bf16[544,256]{1,0:T(8,128)(2,1)}, bf16[544,256]{1,0:T(8,128)(2,1)}, u32[]{:S(2)}, u32[]{:S(2)}) collective-permute-start(bf16[544,256]{1,0:T(8,128)(2,1)} %shard_map.109), channel_id=1, source_target_pairs={{0,34},{1,35},{2,32},{3,33},{4,38},{5,39},{6,36},{7,37},{8,42},{9,... | collective-permute-start | bytes 835592 | tf_op jit(solution)/shard_map/ppermute | solution.py:46
  78.2 4.8 %shard_map.112 = bf16[544,256]{1,0:T(8,128)(2,1)} custom-call(s32[4]{0:T(128)S(1)} %copy-done.8, s32[2]{0:T(128)S(1)} %get-tuple-element.33.counts, s32[8,6]{1,0:T(8,128)S(1)} %copy-done.6, f32[2,64]{1,0:T(2,128)S(1)} %copy-done.7, bf16[1024,128]{1,0:T(8,128)(2,1)} %collective-permute-done.6.refs_0_, bf16[8,768,128]{2,1,0:T(8,128)(2,1)S(1)} %copy-done, ...), custom_call_target="tpu_custom_call" | custom-call | flops 402653184 | bytes 1572864 | tf_op jit(solution)/shard_map/pallas_call | solution.py:154
  83.0 3.2 %collective-permute-start.9 = (bf16[544,256]{1,0:T(8,128)(2,1)}, bf16[544,256]{1,0:T(8,128)(2,1)}, u32[]{:S(2)}, u32[]{:S(2)}) collective-permute-start(bf16[544,256]{1,0:T(8,128)(2,1)} %shard_map.112), channel_id=1, source_target_pairs={{0,192},{1,193},{2,194},{3,195},{4,196},{5,197},{6,198},{7,199},{8... | collective-permute-start | bytes 835592 | tf_op jit(solution)/shard_map/ppermute | solution.py:46
  86.2 3.9 %shard_map.114 = bf16[544,256]{1,0:T(8,128)(2,1)} custom-call(s32[4]{0:T(128)S(1)} %copy-done.8, s32[2]{0:T(128)S(1)} %get-tuple-element.31.counts, s32[8,6]{1,0:T(8,128)S(1)} %copy-done.6, f32[2,64]{1,0:T(2,128)S(1)} %copy-done.7, bf16[1024,128]{1,0:T(8,128)(2,1)S(1)} %collective-permute-done.10.refs_0_, bf16[8,768,128]{2,1,0:T(8,128)(2,1)S(1)} %copy-done, ...), custom_call_target="tpu_custom_call" | custom-call | flops 402653184 | bytes 1572864 | tf_op jit(solution)/shard_map/pallas_call | solution.py:154
  90.1 4.8 %shard_map.116 = bf16[544,256]{1,0:T(8,128)(2,1)} custom-call(s32[4]{0:T(128)S(1)} %copy-done.8, s32[2]{0:T(128)S(1)} %get-tuple-element.36.counts, s32[8,6]{1,0:T(8,128)S(1)} %copy-done.6, f32[2,64]{1,0:T(2,128)S(1)} %copy-done.7, bf16[1024,128]{1,0:T(8,128)(2,1)} %collective-permute-done.14.refs_0_, bf16[8,768,128]{2,1,0:T(8,128)(2,1)S(1)} %copy-done, ...), custom_call_target="tpu_custom_call" | custom-call | flops 402653184 | bytes 1572864 | tf_op jit(solution)/shard_map/pallas_call | solution.py:154
  94.9 2.1 %collective-permute-start.17 = (bf16[544,256]{1,0:T(8,128)(2,1)}, bf16[544,256]{1,0:T(8,128)(2,1)}, u32[]{:S(2)}, u32[]{:S(2)}) collective-permute-start(bf16[544,256]{1,0:T(8,128)(2,1)} %shard_map.116), channel_id=1, source_target_pairs={{0,128},{1,129},{2,130},{3,131},{4,132},{5,133},{6,134},{7,135},{8... | collective-permute-start | bytes 835592 | tf_op jit(solution)/shard_map/ppermute | solution.py:46
  97.9 2.1 %copy.15 = bf16[256,8,128]{0,2,1:T(8,128)(2,1)} copy(bf16[256,8,128]{2,1,0:T(8,128)(2,1)} %param.19) | data formatting | bytes 1048576 | tf_op args[8]
  102.1 2.3 %shard_map.117 = (f32[512,256]{1,0:T(8,128)S(1)}, f32[8,256]{1,0:T(8,128)S(1)}) custom-call(s32[4]{0:T(128)S(1)} %copy-done.8, bf16[1024,128]{1,0:T(8,128)(2,1)S(1)} %bitcast.60, bf16[8,256,128]{2,1,0:T(8,128)(2,1)S(1)} %bitcast.62, bf16[8,128,256]{2,1,0:T(8,128)(2,1)S(1)} %bitcast.63), custom_call_target="tpu_custom_call" | custom-call | flops 134217728 | bytes 786432 | tf_op jit(solution)/shard_map/pallas_call | solution.py:196
  104.4 4.1 %shard_map.110.a_ref = bf16[544,256]{1,0:T(8,128)(2,1)S(1)} custom-call(s32[4]{0:T(128)S(1)} %copy-done.8, s32[2]{0:T(128)S(1)} %get-tuple-element.35.counts, s32[8,6]{1,0:T(8,128)S(1)} %copy-done.6, f32[2,64]{1,0:T(2,128)S(1)} %copy-done.7, bf16[1024,128]{1,0:T(8,128)(2,1)S(1)} %bitcast.61, bf16[8,768,128]{2,1,0:T(8,128)(2,1)S(1)} %copy-done, ...), custom_call_target="tpu_custom_call" | custom-call | flops 402653184 | bytes 1572864 | tf_op jit(solution)/shard_map/pallas_call | solution.py:154
  108.5 1.5 shard_map.118.a_ref
  111.6 3.4 %copy-done.2 = bf16[512,8192]{1,0:T(8,128)(2,1)S(1)} copy-done((bf16[512,8192]{1,0:T(8,128)(2,1)S(1)}, bf16[512,8192]{1,0:T(8,128)(2,1)}, u32[]{:S(2)}) %copy-start.2) | copy-done | bytes 8388632
  115.0 3.6 %shard_map.123 = f32[4,256,256]{2,1,0:T(8,128)S(1)} custom-call(s32[4]{0:T(128)S(1)} %get-tuple-element.13.own_at, s32[4]{0:T(128)S(1)} %get-tuple-element.14.other_at, bf16[256,512]{1,0:T(8,128)(2,1)S(1)} %shard_map.118.a_ref, bf16[256,512]{1,0:T(8,128)(2,1)S(1)} %collective-permute-done.18.b_ref, bf16[512,8192]{1,0:T(8,128)(2,1)S(1)} %copy-done.2, ...), custom_call_target="tpu_custom_call" | custom-call | flops 536870912 | bytes 2097152 | tf_op jit(solution)/shard_map/pallas_call | solution.py:287
  118.6 2.2 %shard_map.124 = bf16[2,256,256]{2,1,0:T(8,128)(2,1)S(1)} custom-call(s32[2]{0:T(128)S(1)} %get-tuple-element.11.own_at, s32[2]{0:T(128)S(1)} %get-tuple-element.12.other_at, bf16[256,512]{1,0:T(8,128)(2,1)S(1)} %shard_map.118.a_ref, bf16[256,512]{1,0:T(8,128)(2,1)S(1)} %collective-permute-done.18.b_ref, bf16[512,8192]{1,0:T(8,128)(2,1)S(1)} %copy-done.2, ...), custom_call_target="tpu_custom_call" | custom-call | flops 268435456 | bytes 1048576 | tf_op jit(solution)/shard_map/pallas_call | solution.py:287
  122.1 4.0 %collective-permute-start.24 = (bf16[1,256,256]{2,1,0:T(8,128)(2,1)S(1)}, bf16[1,256,256]{2,1,0:T(8,128)(2,1)S(1)}, u32[]{:S(2)}, u32[]{:S(2)}) collective-permute-start(bf16[1,256,256]{2,1,0:T(8,128)(2,1)S(1)} %get-tuple-element.28), channel_id=1, source_target_pairs={{0,28},{1,29},{2,30},{3,31},{4,0},{5,1},{6,2},{7,3},{8,4},{9,5},{1... | collective-permute-start | bytes 393224 | tf_op jit(solution)/shard_map/ppermute | solution.py:46
  126.2 3.7 %collective-permute-done.20 = bf16[1,256,256]{2,1,0:T(8,128)(2,1)S(1)} collective-permute-done((bf16[1,256,256]{2,1,0:T(8,128)(2,1)S(1)}, bf16[1,256,256]{2,1,0:T(8,128)(2,1)S(1)}, u32[]{:S(2)}, u32[]{:S(2)}) %collective-permute-start.20) | collective-permute-done | bytes 131104 | tf_op jit(solution)/shard_map/ppermute | solution.py:46
  130.1 3.3 %collective-permute-start.25 = (bf16[2,256,256]{2,1,0:T(8,128)(2,1)S(1)}, bf16[2,256,256]{2,1,0:T(8,128)(2,1)S(1)}, u32[]{:S(2)}, u32[]{:S(2)}) collective-permute-start(bf16[2,256,256]{2,1,0:T(8,128)(2,1)S(1)} %pad_maximum_fusion.1), channel_id=1, source_target_pairs={{0,28},{1,29},{2,30},{3,31},{4,0},{5,1},{6,2},{7,3},{8,4},{9,5},{1... | collective-permute-start | bytes 786440 | tf_op jit(solution)/shard_map/ppermute | solution.py:46
  133.4 3.6 %shard_map.122 = f32[4,256,256]{2,1,0:T(8,128)S(1)} custom-call(s32[4]{0:T(128)S(1)} %get-tuple-element.39.own_at, s32[4]{0:T(128)S(1)} %get-tuple-element.40.other_at, bf16[256,512]{1,0:T(8,128)(2,1)S(1)} %shard_map.118.a_ref, bf16[256,512]{1,0:T(8,128)(2,1)S(1)} %collective-permute-done.18.b_ref, bf16[512,8192]{1,0:T(8,128)(2,1)S(1)} %copy-done.2, ...), custom_call_target="tpu_custom_call" | custom-call | flops 536870912 | bytes 2097152 | tf_op jit(solution)/shard_map/pallas_call | solution.py:287
  136.9 2.1 %collective-permute-done.21 = bf16[2,256,256]{2,1,0:T(8,128)(2,1)S(1)} collective-permute-done((bf16[2,256,256]{2,1,0:T(8,128)(2,1)S(1)}, bf16[2,256,256]{2,1,0:T(8,128)(2,1)S(1)}, u32[]{:S(2)}, u32[]{:S(2)}) %collective-permute-start.21) | collective-permute-done | bytes 262176 | tf_op jit(solution)/shard_map/ppermute | solution.py:46
  139.2 2.0 %collective-permute-start.22 = (bf16[2,256,256]{2,1,0:T(8,128)(2,1)S(1)}, bf16[2,256,256]{2,1,0:T(8,128)(2,1)S(1)}, u32[]{:S(2)}, u32[]{:S(2)}) collective-permute-start(bf16[2,256,256]{2,1,0:T(8,128)(2,1)S(1)} %get-tuple-element.21), channel_id=1, source_target_pairs={{0,4},{1,5},{2,6},{3,7},{4,8},{5,9},{6,10},{7,11},{8,12},{9,13},{1... | collective-permute-start | bytes 786440 | tf_op jit(solution)/shard_map/ppermute | solution.py:46
  141.2 1.3 collective-permute-start.26
  142.6 3.4 %copy-done.3 = bf16[512,8192]{1,0:T(8,128)(2,1)S(1)} copy-done((bf16[512,8192]{1,0:T(8,128)(2,1)S(1)}, bf16[512,8192]{1,0:T(8,128)(2,1)}, u32[]{:S(2)}) %copy-start.3) | copy-done | bytes 8388632
  146.0 3.6 %shard_map.121 = f32[4,256,256]{2,1,0:T(8,128)S(1)} custom-call(s32[4]{0:T(128)S(1)} %get-tuple-element.17.own_at, s32[4]{0:T(128)S(1)} %get-tuple-element.18.other_at, bf16[256,512]{1,0:T(8,128)(2,1)S(1)} %shard_map.118.a_ref, bf16[256,512]{1,0:T(8,128)(2,1)S(1)} %collective-permute-done.18.b_ref, bf16[512,8192]{1,0:T(8,128)(2,1)S(1)} %copy-done.3, ...), custom_call_target="tpu_custom_call" | custom-call | flops 536870912 | bytes 2097152 | tf_op jit(solution)/shard_map/pallas_call | solution.py:287
  149.8 1.9 %collective-permute-start.27 = (bf16[2,256,256]{2,1,0:T(8,128)(2,1)S(1)}, bf16[2,256,256]{2,1,0:T(8,128)(2,1)S(1)}, u32[]{:S(2)}, u32[]{:S(2)}) collective-permute-start(bf16[2,256,256]{2,1,0:T(8,128)(2,1)S(1)} %get-tuple-element.20), channel_id=1, source_target_pairs={{0,28},{1,29},{2,30},{3,31},{4,0},{5,1},{6,2},{7,3},{8,4},{9,5},{1... | collective-permute-start | bytes 786440 | tf_op jit(solution)/shard_map/ppermute | solution.py:46
  151.9 2.2 %shard_map.120 = f32[2,256,256]{2,1,0:T(8,128)S(1)} custom-call(s32[2]{0:T(128)S(1)} %get-tuple-element.37.own_at, s32[2]{0:T(128)S(1)} %get-tuple-element.38.other_at, bf16[256,512]{1,0:T(8,128)(2,1)S(1)} %shard_map.118.a_ref, bf16[256,512]{1,0:T(8,128)(2,1)S(1)} %collective-permute-done.18.b_ref, bf16[512,8192]{1,0:T(8,128)(2,1)S(1)} %copy-done.3, ...), custom_call_target="tpu_custom_call" | custom-call | flops 268435456 | bytes 1048576 | tf_op jit(solution)/shard_map/pallas_call | solution.py:287
  154.1 2.2 %collective-permute-done.27 = bf16[2,256,256]{2,1,0:T(8,128)(2,1)S(1)} collective-permute-done((bf16[2,256,256]{2,1,0:T(8,128)(2,1)S(1)}, bf16[2,256,256]{2,1,0:T(8,128)(2,1)S(1)}, u32[]{:S(2)}, u32[]{:S(2)}) %collective-permute-start.27) | collective-permute-done | bytes 262176 | tf_op jit(solution)/shard_map/ppermute | solution.py:46
  156.2 3.0 %collective-permute-done.23 = bf16[2,256,256]{2,1,0:T(8,128)(2,1)S(1)} collective-permute-done((bf16[2,256,256]{2,1,0:T(8,128)(2,1)S(1)}, bf16[2,256,256]{2,1,0:T(8,128)(2,1)S(1)}, u32[]{:S(2)}, u32[]{:S(2)}) %collective-permute-start.23) | collective-permute-done | bytes 262176 | tf_op jit(solution)/shard_map/ppermute | solution.py:46
  159.5 5.0 %collective-permute-done.28 = bf16[256,256]{1,0:T(8,128)(2,1)S(1)} collective-permute-done((bf16[256,256]{1,0:T(8,128)(2,1)S(1)}, bf16[256,256]{1,0:T(8,128)(2,1)S(1)}, u32[]{:S(2)}, u32[]{:S(2)}) %collective-permute-start.28) | collective-permute-done | bytes 131104 | tf_op jit(solution)/shard_map/ppermute | solution.py:46
  (71 shorter events, 11.1 us)
Async XLA Ops:
  0.0 3.4 %copy-start.1 = (bf16[512,8192]{1,0:T(8,128)(2,1)S(1)}, bf16[512,8192]{1,0:T(8,128)(2,1)}, u32[]{:S(2)}) copy-start(bf16[512,8192]{1,0:T(8,128)(2,1)} %w_ref.11) | copy-start | bytes 25165828
  3.4 6.4 %copy-start.10 = (bf16[256,4,128]{2,1,0:T(4,128)(2,1)S(1)}, bf16[256,4,128]{2,1,0:T(4,128)(2,1)}, u32[]{:S(2)}) copy-start(bf16[256,4,128]{2,1,0:T(4,128)(2,1)} %param.11) | copy-start | bytes 786436
  3.4 22.1 %copy-start.8 = (s32[4]{0:T(128)S(1)}, s32[4]{0:T(128)}, u32[]{:S(2)}) copy-start(s32[4]{0:T(128)} %groups.9) | copy-start | bytes 52
  3.4 48.5 %copy-start.11 = (s32[16]{0:T(128)S(1)}, s32[16]{0:T(128)}, u32[]{:S(2)}) copy-start(s32[16]{0:T(128)} %param.17) | copy-start | bytes 196
  3.4 48.6 %copy-start.6 = (s32[8,6]{1,0:T(8,128)S(1)}, s32[8,6]{1,0:T(8,128)}, u32[]{:S(2)}) copy-start(s32[8,6]{1,0:T(8,128)} %scale_index.15) | copy-start | bytes 580
  3.4 48.6 %copy-start.7 = (f32[2,64]{1,0:T(2,128)S(1)}, f32[2,64]{1,0:T(2,128)}, u32[]{:S(2)}) copy-start(f32[2,64]{1,0:T(2,128)} %scale_table.15) | copy-start | bytes 1540
  9.8 42.3 %copy-start = (bf16[8,768,128]{2,1,0:T(8,128)(2,1)S(1)}, bf16[8,768,128]{2,1,0:T(8,128)(2,1)}, u32[]{:S(2)}) copy-start(bf16[8,768,128]{2,1,0:T(8,128)(2,1)} %refs_2_.15) | copy-start | bytes 4718596
  9.8 101.9 %collective-permute-start.19 = (bf16[16,512,256]{2,1,0:T(8,128)(2,1)}, bf16[16,512,256]{2,1,0:T(8,128)(2,1)}, u32[]{:S(2)}, u32[]{:S(2)}) collective-permute-start(bf16[16,512,256]{2,1,0:T(8,128)(2,1)} %shard_map.119), channel_id=1, source_target_pairs={{0,1},{1,0},{2,3},{3,2},{4,5},{5,4},{6,7},{7,6},{8,9},{9,8},{10,11... | collective-permute-start | bytes 12582920 | tf_op jit(solution)/shard_map/ppermute | solution.py:46
  9.8 10.1 %collective-permute-start.4 = (bf16[1024,128]{1,0:T(8,128)(2,1)S(1)}, bf16[1024,128]{1,0:T(8,128)(2,1)}, u32[]{:S(2)}, u32[]{:S(2)}) collective-permute-start(bf16[1024,128]{1,0:T(8,128)(2,1)S(1)} %bitcast.56), channel_id=1, source_target_pairs={{0,34},{1,35},{2,32},{3,33},{4,38},{5,39},{6,36},{7,37},{8,42},{9,... | collective-permute-start | bytes 786440 | tf_op jit(solution)/shard_map/ppermute | solution.py:46
  12.7 10.2 %collective-permute-start.14 = (bf16[1024,128]{1,0:T(8,128)(2,1)S(1)}, bf16[1024,128]{1,0:T(8,128)(2,1)}, u32[]{:S(2)}, u32[]{:S(2)}) collective-permute-start(bf16[1024,128]{1,0:T(8,128)(2,1)S(1)} %bitcast.57), channel_id=1, source_target_pairs={{0,128},{1,129},{2,130},{3,131},{4,132},{5,133},{6,134},{7,135},{8... | collective-permute-start | bytes 786440 | tf_op jit(solution)/shard_map/ppermute | solution.py:46
  19.9 32.1 %collective-permute-start.7 = (bf16[1024,128]{1,0:T(8,128)(2,1)}, bf16[1024,128]{1,0:T(8,128)(2,1)}, u32[]{:S(2)}, u32[]{:S(2)}) collective-permute-start(bf16[1024,128]{1,0:T(8,128)(2,1)} %collective-permute-done.4.refs_0_), channel_id=1, source_target_pairs={{0,64},{1,65},{2,66},{3,67},{4,68},{5,69},{6,70},{7,71},{8,72},{9,... | collective-permute-start | bytes 786440 | tf_op jit(solution)/shard_map/ppermute | solution.py:46
  22.2 35.9 %collective-permute-start.11 = (bf16[1024,128]{1,0:T(8,128)(2,1)}, bf16[1024,128]{1,0:T(8,128)(2,1)}, u32[]{:S(2)}, u32[]{:S(2)}) collective-permute-start(bf16[1024,128]{1,0:T(8,128)(2,1)} %collective-permute-done.4.refs_0_), channel_id=1, source_target_pairs={{0,192},{1,193},{2,194},{3,195},{4,196},{5,197},{6,198},{7,199},{8... | collective-permute-start | bytes 786440 | tf_op jit(solution)/shard_map/ppermute | solution.py:46
  22.8 40.7 %collective-permute-start.15 = (bf16[1024,128]{1,0:T(8,128)(2,1)}, bf16[1024,128]{1,0:T(8,128)(2,1)}, u32[]{:S(2)}, u32[]{:S(2)}) collective-permute-start(bf16[1024,128]{1,0:T(8,128)(2,1)} %collective-permute-done.14.refs_0_), channel_id=1, source_target_pairs={{0,34},{1,35},{2,32},{3,33},{4,38},{5,39},{6,36},{7,37},{8,42},{9,... | collective-permute-start | bytes 786440 | tf_op jit(solution)/shard_map/ppermute | solution.py:46
  25.5 6.5 %collective-permute-start = (s32[5]{0:T(128)S(1)}, s32[5]{0:T(128)S(1)}, u32[]{:S(2)}, u32[]{:S(2)}) collective-permute-start(s32[5]{0:T(128)S(1)} %pad_add_fusion.1), channel_id=1, source_target_pairs={{0,34},{1,35},{2,32},{3,33},{4,38},{5,39},{6,36},{7,37},{8,42},{9,... | collective-permute-start | bytes 68 | tf_op jit(solution)/shard_map/ppermute | solution.py:46
  33.1 4.7 %collective-permute-start.1 = (s32[1]{0:T(128)}, s32[1]{0:T(128)}, u32[]{:S(2)}, u32[]{:S(2)}) collective-permute-start(s32[1]{0:T(128)} %add.259), channel_id=1, source_target_pairs={{0,64},{1,65},{2,66},{3,67},{4,68},{5,69},{6,70},{7,71},{8,72},{9,... | collective-permute-start | bytes 20 | tf_op jit(solution)/shard_map/ppermute | solution.py:46
  37.8 4.5 %collective-permute-start.2 = (s32[1]{0:T(128)}, s32[1]{0:T(128)}, u32[]{:S(2)}, u32[]{:S(2)}) collective-permute-start(s32[1]{0:T(128)} %add.259), channel_id=1, source_target_pairs={{0,192},{1,193},{2,194},{3,195},{4,196},{5,197},{6,198},{7,199},{8... | collective-permute-start | bytes 20 | tf_op jit(solution)/shard_map/ppermute | solution.py:46
  42.3 5.2 %collective-permute-start.3 = (s32[1]{0:T(128)}, s32[1]{0:T(128)}, u32[]{:S(2)}, u32[]{:S(2)}) collective-permute-start(s32[1]{0:T(128)} %add.259), channel_id=1, source_target_pairs={{0,128},{1,129},{2,130},{3,131},{4,132},{5,133},{6,134},{7,135},{8... | collective-permute-start | bytes 20 | tf_op jit(solution)/shard_map/ppermute | solution.py:46
  47.5 22.6 %collective-permute-start.6 = (bf16[1024,128]{1,0:T(8,128)(2,1)S(1)}, bf16[1024,128]{1,0:T(8,128)(2,1)}, u32[]{:S(2)}, u32[]{:S(2)}) collective-permute-start(bf16[1024,128]{1,0:T(8,128)(2,1)S(1)} %bitcast.58), channel_id=1, source_target_pairs={{0,64},{1,65},{2,66},{3,67},{4,68},{5,69},{6,70},{7,71},{8,72},{9,... | collective-permute-start | bytes 786440 | tf_op jit(solution)/shard_map/ppermute | solution.py:46
  56.1 19.9 %collective-permute-start.8 = (bf16[544,256]{1,0:T(8,128)(2,1)S(1)}, bf16[544,256]{1,0:T(8,128)(2,1)S(1)}, u32[]{:S(2)}, u32[]{:S(2)}) collective-permute-start(bf16[544,256]{1,0:T(8,128)(2,1)S(1)} %shard_map.111), channel_id=1, source_target_pairs={{0,34},{1,35},{2,32},{3,33},{4,38},{5,39},{6,36},{7,37},{8,42},{9,... | collective-permute-start | bytes 835592 | tf_op jit(solution)/shard_map/ppermute | solution.py:46
  58.1 24.9 %collective-permute-start.10 = (bf16[1024,128]{1,0:T(8,128)(2,1)S(1)}, bf16[1024,128]{1,0:T(8,128)(2,1)S(1)}, u32[]{:S(2)}, u32[]{:S(2)}) collective-permute-start(bf16[1024,128]{1,0:T(8,128)(2,1)S(1)} %bitcast.59), channel_id=1, source_target_pairs={{0,192},{1,193},{2,194},{3,195},{4,196},{5,197},{6,198},{7,199},{8... | collective-permute-start | bytes 786440 | tf_op jit(solution)/shard_map/ppermute | solution.py:46
  63.5 22.7 %collective-permute-start.12 = (bf16[544,256]{1,0:T(8,128)(2,1)S(1)}, bf16[544,256]{1,0:T(8,128)(2,1)S(1)}, u32[]{:S(2)}, u32[]{:S(2)}) collective-permute-start(bf16[544,256]{1,0:T(8,128)(2,1)S(1)} %shard_map.113), channel_id=1, source_target_pairs={{0,34},{1,35},{2,32},{3,33},{4,38},{5,39},{6,36},{7,37},{8,42},{9,... | collective-permute-start | bytes 835592 | tf_op jit(solution)/shard_map/ppermute | solution.py:46
  70.1 20.0 %collective-permute-start.16 = (bf16[544,256]{1,0:T(8,128)(2,1)S(1)}, bf16[544,256]{1,0:T(8,128)(2,1)S(1)}, u32[]{:S(2)}, u32[]{:S(2)}) collective-permute-start(bf16[544,256]{1,0:T(8,128)(2,1)S(1)} %shard_map.115), channel_id=1, source_target_pairs={{0,34},{1,35},{2,32},{3,33},{4,38},{5,39},{6,36},{7,37},{8,42},{9,... | collective-permute-start | bytes 835592 | tf_op jit(solution)/shard_map/ppermute | solution.py:46
  76.0 28.3 %collective-permute-start.5 = (bf16[544,256]{1,0:T(8,128)(2,1)}, bf16[544,256]{1,0:T(8,128)(2,1)}, u32[]{:S(2)}, u32[]{:S(2)}) collective-permute-start(bf16[544,256]{1,0:T(8,128)(2,1)} %shard_map.109), channel_id=1, source_target_pairs={{0,34},{1,35},{2,32},{3,33},{4,38},{5,39},{6,36},{7,37},{8,42},{9,... | collective-permute-start | bytes 835592 | tf_op jit(solution)/shard_map/ppermute | solution.py:46
  83.0 25.5 %collective-permute-start.9 = (bf16[544,256]{1,0:T(8,128)(2,1)}, bf16[544,256]{1,0:T(8,128)(2,1)}, u32[]{:S(2)}, u32[]{:S(2)}) collective-permute-start(bf16[544,256]{1,0:T(8,128)(2,1)} %shard_map.112), channel_id=1, source_target_pairs={{0,192},{1,193},{2,194},{3,195},{4,196},{5,197},{6,198},{7,199},{8... | collective-permute-start | bytes 835592 | tf_op jit(solution)/shard_map/ppermute | solution.py:46
  90.1 6.9 %copy-start.9 = (bf16[256,8,128]{2,1,0:T(8,128)(2,1)S(1)}, bf16[256,8,128]{2,1,0:T(8,128)(2,1)}, u32[]{:S(2)}) copy-start(bf16[256,8,128]{2,1,0:T(8,128)(2,1)} %param.18) | copy-start | bytes 1572868
  90.1 18.4 %collective-permute-start.13 = (bf16[544,256]{1,0:T(8,128)(2,1)}, bf16[544,256]{1,0:T(8,128)(2,1)}, u32[]{:S(2)}, u32[]{:S(2)}) collective-permute-start(bf16[544,256]{1,0:T(8,128)(2,1)} %shard_map.114), channel_id=1, source_target_pairs={{0,64},{1,65},{2,66},{3,67},{4,68},{5,69},{6,70},{7,71},{8,72},{9,... | collective-permute-start | bytes 835592 | tf_op jit(solution)/shard_map/ppermute | solution.py:46
  94.9 13.6 %collective-permute-start.17 = (bf16[544,256]{1,0:T(8,128)(2,1)}, bf16[544,256]{1,0:T(8,128)(2,1)}, u32[]{:S(2)}, u32[]{:S(2)}) collective-permute-start(bf16[544,256]{1,0:T(8,128)(2,1)} %shard_map.116), channel_id=1, source_target_pairs={{0,128},{1,129},{2,130},{3,131},{4,132},{5,133},{6,134},{7,135},{8... | collective-permute-start | bytes 835592 | tf_op jit(solution)/shard_map/ppermute | solution.py:46
  100.0 1.0 copy-start.4
  101.0 1.0 copy-start.5
  110.0 1.6 collective-permute-start.18
  111.6 3.4 %copy-start.2 = (bf16[512,8192]{1,0:T(8,128)(2,1)S(1)}, bf16[512,8192]{1,0:T(8,128)(2,1)}, u32[]{:S(2)}) copy-start(bf16[512,8192]{1,0:T(8,128)(2,1)} %w_ref.11) | copy-start | bytes 25165828
  120.9 9.0 %collective-permute-start.20 = (bf16[1,256,256]{2,1,0:T(8,128)(2,1)S(1)}, bf16[1,256,256]{2,1,0:T(8,128)(2,1)S(1)}, u32[]{:S(2)}, u32[]{:S(2)}) collective-permute-start(bf16[1,256,256]{2,1,0:T(8,128)(2,1)S(1)} %get-tuple-element.27), channel_id=1, source_target_pairs={{0,4},{1,5},{2,6},{3,7},{4,8},{5,9},{6,10},{7,11},{8,12},{9,13},{1... | collective-permute-start | bytes 393224 | tf_op jit(solution)/shard_map/ppermute | solution.py:46
  122.1 7.7 %collective-permute-start.24 = (bf16[1,256,256]{2,1,0:T(8,128)(2,1)S(1)}, bf16[1,256,256]{2,1,0:T(8,128)(2,1)S(1)}, u32[]{:S(2)}, u32[]{:S(2)}) collective-permute-start(bf16[1,256,256]{2,1,0:T(8,128)(2,1)S(1)} %get-tuple-element.28), channel_id=1, source_target_pairs={{0,28},{1,29},{2,30},{3,31},{4,0},{5,1},{6,2},{7,3},{8,4},{9,5},{1... | collective-permute-start | bytes 393224 | tf_op jit(solution)/shard_map/ppermute | solution.py:46
  129.9 9.1 %collective-permute-start.21 = (bf16[2,256,256]{2,1,0:T(8,128)(2,1)S(1)}, bf16[2,256,256]{2,1,0:T(8,128)(2,1)S(1)}, u32[]{:S(2)}, u32[]{:S(2)}) collective-permute-start(bf16[2,256,256]{2,1,0:T(8,128)(2,1)S(1)} %pad_maximum_fusion), channel_id=1, source_target_pairs={{0,4},{1,5},{2,6},{3,7},{4,8},{5,9},{6,10},{7,11},{8,12},{9,13},{1... | collective-permute-start | bytes 786440 | tf_op jit(solution)/shard_map/ppermute | solution.py:46
  130.1 9.0 %collective-permute-start.25 = (bf16[2,256,256]{2,1,0:T(8,128)(2,1)S(1)}, bf16[2,256,256]{2,1,0:T(8,128)(2,1)S(1)}, u32[]{:S(2)}, u32[]{:S(2)}) collective-permute-start(bf16[2,256,256]{2,1,0:T(8,128)(2,1)S(1)} %pad_maximum_fusion.1), channel_id=1, source_target_pairs={{0,28},{1,29},{2,30},{3,31},{4,0},{5,1},{6,2},{7,3},{8,4},{9,5},{1... | collective-permute-start | bytes 786440 | tf_op jit(solution)/shard_map/ppermute | solution.py:46
  139.2 10.4 %collective-permute-start.22 = (bf16[2,256,256]{2,1,0:T(8,128)(2,1)S(1)}, bf16[2,256,256]{2,1,0:T(8,128)(2,1)S(1)}, u32[]{:S(2)}, u32[]{:S(2)}) collective-permute-start(bf16[2,256,256]{2,1,0:T(8,128)(2,1)S(1)} %get-tuple-element.21), channel_id=1, source_target_pairs={{0,4},{1,5},{2,6},{3,7},{4,8},{5,9},{6,10},{7,11},{8,12},{9,13},{1... | collective-permute-start | bytes 786440 | tf_op jit(solution)/shard_map/ppermute | solution.py:46
  141.2 8.4 %collective-permute-start.26 = (bf16[2,256,256]{2,1,0:T(8,128)(2,1)S(1)}, bf16[2,256,256]{2,1,0:T(8,128)(2,1)S(1)}, u32[]{:S(2)}, u32[]{:S(2)}) collective-permute-start(bf16[2,256,256]{2,1,0:T(8,128)(2,1)S(1)} %get-tuple-element.22), channel_id=1, source_target_pairs={{0,28},{1,29},{2,30},{3,31},{4,0},{5,1},{6,2},{7,3},{8,4},{9,5},{1... | collective-permute-start | bytes 786440 | tf_op jit(solution)/shard_map/ppermute | solution.py:46
  142.6 3.4 %copy-start.3 = (bf16[512,8192]{1,0:T(8,128)(2,1)S(1)}, bf16[512,8192]{1,0:T(8,128)(2,1)}, u32[]{:S(2)}) copy-start(bf16[512,8192]{1,0:T(8,128)(2,1)} %w_ref.11) | copy-start | bytes 25165828
  149.8 6.5 %collective-permute-start.27 = (bf16[2,256,256]{2,1,0:T(8,128)(2,1)S(1)}, bf16[2,256,256]{2,1,0:T(8,128)(2,1)S(1)}, u32[]{:S(2)}, u32[]{:S(2)}) collective-permute-start(bf16[2,256,256]{2,1,0:T(8,128)(2,1)S(1)} %get-tuple-element.20), channel_id=1, source_target_pairs={{0,28},{1,29},{2,30},{3,31},{4,0},{5,1},{6,2},{7,3},{8,4},{9,5},{1... | collective-permute-start | bytes 786440 | tf_op jit(solution)/shard_map/ppermute | solution.py:46
  151.7 7.6 %collective-permute-start.23 = (bf16[2,256,256]{2,1,0:T(8,128)(2,1)S(1)}, bf16[2,256,256]{2,1,0:T(8,128)(2,1)S(1)}, u32[]{:S(2)}, u32[]{:S(2)}) collective-permute-start(bf16[2,256,256]{2,1,0:T(8,128)(2,1)S(1)} %get-tuple-element.19), channel_id=1, source_target_pairs={{0,4},{1,5},{2,6},{3,7},{4,8},{5,9},{6,10},{7,11},{8,12},{9,13},{1... | collective-permute-start | bytes 786440 | tf_op jit(solution)/shard_map/ppermute | solution.py:46
  159.4 5.1 %collective-permute-start.28 = (bf16[256,256]{1,0:T(8,128)(2,1)S(1)}, bf16[256,256]{1,0:T(8,128)(2,1)S(1)}, u32[]{:S(2)}, u32[]{:S(2)}) collective-permute-start(bf16[256,256]{1,0:T(8,128)(2,1)S(1)} %fusion.8), channel_id=1, source_target_pairs={{0,2},{1,3},{2,0},{3,1},{4,6},{5,7},{6,4},{7,5},{8,10},{9,11},{10,... | collective-permute-start | bytes 393224 | tf_op jit(solution)/shard_map/ppermute | solution.py:46

commit v2 on v1

v2 whole, which is shorter than its diff:
```python
import functools
import math

import jax
import jax.numpy as jnp
from jax import lax
from jax.experimental import pallas as pl
from jax.experimental.pallas import tpu as pltpu
from jax.sharding import PartitionSpec as P

SPAN = 128
SBLK = 128
HEADS = 4
ROWS = 256
DH = 128
SLOTS = 768
BLOCKS = SLOTS // SBLK
PART_ROWS = HEADS * DH
LSE_ROWS = 32
MSG_ROWS = PART_ROWS + LSE_ROWS
FLOOR = -1e30
LOG2E = math.log2(math.e)
INVERSE = 1.0 / math.sqrt(DH)
AXES = ("ctx", "head")
F32, BF16, I32 = jnp.float32, jnp.bfloat16, jnp.int32
VMEM_LIMIT = 20 * 1024 * 1024


def linear(y, xh, z, xl, core):
    return (((y % 4) * 2 + xh % 2) * 8 + z % 8) * 4 + (xl % 2) * 2 + core % 2


def moved(dy=0, dxh=0, dz=0, dxl=0, dcore=0):
    return [
        (linear(y, xh, z, xl, c), linear(y + dy, xh + dxh, z + dz, xl + dxl, c + dcore))
        for y in range(4)
        for xh in range(2)
        for z in range(8)
        for xl in range(2)
        for c in range(2)
    ]


def send(value, **move):
    return lax.ppermute(value, AXES, moved(**move))


def params():
    return pltpu.CompilerParams(vmem_limit_bytes=VMEM_LIMIT)


def fixed(value, space=pltpu.VMEM):
    return pltpu.with_memory_space_constraint(value, space)


def log2(value):
    return jnp.log(value) * LOG2E


def pack_lse(lse8):
    high = lse8.astype(BF16).astype(F32)
    rest = lse8 - high
    middle = rest.astype(BF16).astype(F32)
    low = (rest - middle).astype(BF16).astype(F32)
    return jnp.concatenate([high, middle, low, jnp.zeros_like(low)], axis=0).astype(BF16)


def unpack_lse(packed):
    wide = packed.astype(F32)
    return wide[0:8] + wide[8:16] + wide[16:24]


def history_kernel(blocks, at, groups, counts, scale_index, scale_table, *refs):
    q_refs, (k_ref, v_ref, *rest) = refs[:blocks], refs[blocks:]
    if at is not None:
        prev_ref, out_ref, weights_ref = rest
    else:
        out_ref, weights_ref = rest
    lane = lax.broadcasted_iota(I32, (1, ROWS), 1)
    slot = lax.broadcasted_iota(I32, (SBLK, ROWS), 0)
    units = [(block, head) for block in range(blocks) for head in range(HEADS)]

    def products(unit):
        block, head = units[unit]
        return lax.dot_general(
            k_ref[groups[head]],
            q_refs[block][head * ROWS : (head + 1) * ROWS, :],
            (((1,), (1,)), ((), ())),
            preferred_element_type=F32,
        )

    following = products(0)
    for unit, (block, head) in enumerate(units):
        if head == 0:
            lses = []
            count = jnp.where(lane < SPAN, counts[2 * block], counts[2 * block + 1])
            seen = count > 0
            if at is not None:
                held = unpack_lse(prev_ref[at, PART_ROWS:, :])
        group = groups[head]
        raw = following
        if unit + 1 < len(units):
            following = products(unit + 1)
        scores = []
        for part in range(BLOCKS):
            scale = scale_table[0, scale_index[group, part]] * (INVERSE * LOG2E)
            piece = raw[part * SBLK : (part + 1) * SBLK] * scale
            scores.append(jnp.where(slot < count - part * SBLK, piece, FLOOR))
        top = functools.reduce(jnp.maximum, scores)
        top = jnp.max(top, axis=0, keepdims=True)
        total = jnp.zeros((SBLK, ROWS), F32)
        for part in range(BLOCKS):
            scale = scale_table[1, scale_index[group, part]]
            expo = jnp.exp2(scores[part] - top)
            total = total + expo
            weights_ref[head, part * SBLK : (part + 1) * SBLK, :] = (expo * scale).astype(BF16)
        total = jnp.sum(total, axis=0, keepdims=True)
        mixed = times_transposed(v_ref[group], weights_ref[head])
        lse = jnp.where(seen, top + log2(total), FLOOR)
        share = jnp.where(seen, 1.0 / total, 0.0)
        rows = slice(head * DH, (head + 1) * DH)
        if at is not None:
            before = held[head : head + 1]
            peak = jnp.maximum(lse, before)
            mine = jnp.exp2(lse - peak)
            other = jnp.exp2(before - peak)
            both = mine + other
            inverse = 1.0 / both
            mixed = mixed * (share * mine * inverse)
            mixed = mixed + prev_ref[at, rows, :].astype(F32) * (other * inverse)
            lse = peak + log2(both)
        else:
            mixed = mixed * share
        out_ref[block, rows, :] = mixed.astype(BF16)
        lses.append(lse)
        if head == HEADS - 1:
            lses.append(jnp.zeros((8 - HEADS, ROWS), F32))
            out_ref[block, PART_ROWS:, :] = pack_lse(jnp.concatenate(lses, axis=0))


def times_transposed(values, weights):
    return lax.dot_general(
        values, weights, (((0,), (0,)), ((), ())), preferred_element_type=F32
    )


def in_vmem():
    return pl.BlockSpec(memory_space=pltpu.VMEM)


def in_smem():
    return pl.BlockSpec(memory_space=pltpu.SMEM)


def history(groups, counts, scale_index, scale_table, queries, keys, values, previous=None):
    blocks = len(queries)
    operands = [*queries, keys, values]
    at = None
    if previous is not None:
        held, at = previous
        operands.append(held)
    return pl.pallas_call(
        functools.partial(history_kernel, blocks, at),
        out_shape=jax.ShapeDtypeStruct((blocks, MSG_ROWS, ROWS), BF16),
        in_specs=[in_smem()] * 4 + [in_vmem()] * len(operands),
        out_specs=in_vmem(),
        scratch_shapes=[pltpu.VMEM((HEADS, SLOTS, ROWS), BF16)],
        compiler_params=params(),
        cost_estimate=pl.CostEstimate(
            flops=4 * blocks * HEADS * ROWS * SLOTS * DH,
            bytes_accessed=2 * HEADS * SLOTS * DH * 2,
            transcendentals=blocks * HEADS * ROWS * SLOTS,
        ),
    )(groups, counts, scale_index, scale_table, *operands)


def fresh_kernel(groups, q_ref, k_ref, v_ref, out_ref, lse_ref):
    column = lax.broadcasted_iota(I32, (ROWS, ROWS), 0)
    row = lax.broadcasted_iota(I32, (ROWS, ROWS), 1)
    visible = (column <= row) & ((column >= SPAN) | (row < SPAN))
    lses = []
    for head in range(HEADS):
        group = groups[head]
        raw = lax.dot_general(
            k_ref[group],
            q_ref[head * ROWS : (head + 1) * ROWS, :],
            (((1,), (1,)), ((), ())),
            preferred_element_type=F32,
        )
        score = jnp.where(visible, raw * (INVERSE * LOG2E), FLOOR)
        top = jnp.max(score, axis=0, keepdims=True)
        expo = jnp.exp2(score - top)
        total = jnp.sum(expo, axis=0, keepdims=True)
        mixed = times_transposed(v_ref[group], expo.astype(BF16))
        out_ref[head * DH : (head + 1) * DH, :] = mixed * (1.0 / total)
        lses.append(top + log2(total))
    lses.append(jnp.zeros((8 - HEADS, ROWS), F32))
    lse_ref[...] = jnp.concatenate(lses, axis=0)


def fresh_part(groups, query, new_keys, new_values):
    return pl.pallas_call(
        fresh_kernel,
        out_shape=(
            jax.ShapeDtypeStruct((PART_ROWS, ROWS), F32),
            jax.ShapeDtypeStruct((8, ROWS), F32),
        ),
        in_specs=[in_smem()] + [in_vmem()] * 3,
        out_specs=(in_vmem(), in_vmem()),
        compiler_params=params(),
        cost_estimate=pl.CostEstimate(
            flops=4 * HEADS * ROWS * ROWS * DH,
            bytes_accessed=HEADS * ROWS * DH * 6,
            transcendentals=HEADS * ROWS * ROWS,
        ),
    )(groups, query, new_keys, new_values)


def combine_kernel(a_ref, b_ref, c_ref, d_ref, fresh_ref, fresh_lse_ref, out_ref):
    parts = (a_ref, b_ref, c_ref, d_ref)
    lses = [unpack_lse(part[0, PART_ROWS:, :]) for part in parts]
    fresh_lse = fresh_lse_ref[...]
    peak = functools.reduce(jnp.maximum, lses, fresh_lse)
    weights = [jnp.exp2(lse - peak) for lse in lses]
    fresh_weight = jnp.exp2(fresh_lse - peak)
    inverse = 1.0 / functools.reduce(jnp.add, weights, fresh_weight)
    weights = [weight * inverse for weight in weights]
    fresh_weight = fresh_weight * inverse
    for head in range(HEADS):
        rows = slice(head * DH, (head + 1) * DH)
        total = fresh_ref[rows, :] * fresh_weight[head : head + 1]
        for part, weight in zip(parts, weights):
            total = total + part[0, rows, :].astype(F32) * weight[head : head + 1]
        out_ref[:, rows] = jnp.transpose(total).astype(BF16)


def combined(parts, fresh, fresh_lse):
    return pl.pallas_call(
        combine_kernel,
        out_shape=jax.ShapeDtypeStruct((ROWS, PART_ROWS), BF16),
        in_specs=[pl.BlockSpec(memory_space=pltpu.VMEM)] * 6,
        out_specs=pl.BlockSpec(memory_space=pltpu.VMEM),
        compiler_params=params(),
        cost_estimate=pl.CostEstimate(
            flops=10 * ROWS * PART_ROWS, bytes_accessed=3 * 2**20, transcendentals=0
        ),
    )(*parts, fresh, fresh_lse)


def load_kernel(core, *refs):
    (*whole_in, weight), outs, sems = refs[: len(refs) // 2], refs[len(refs) // 2 : -1], refs[-1]
    pairs = []
    for source, target in zip(whole_in, outs):
        for group in range(source.shape[0]):
            pairs.append((source.at[group], target.at[group]))
    for block in range(outs[-1].shape[0]):
        columns = pl.ds(pl.multiple_of((2 * block + core[0]) * ROWS, ROWS), ROWS)
        pairs.append((weight.at[:, columns], outs[-1].at[block]))
    copies = [
        pltpu.make_async_copy(source, target, sems.at[place])
        for place, (source, target) in enumerate(pairs)
    ]
    for copy in copies:
        copy.start()
    for copy in copies:
        copy.wait()


def loaded(core, weight, *whole):
    depth, width = weight.shape
    count = width // (2 * ROWS)
    shapes = [value.shape for value in whole] + [(count, depth, ROWS)]
    total = count + sum(value.shape[0] for value in whole)
    return pl.pallas_call(
        load_kernel,
        out_shape=[pltpu.VMEM(shape, BF16) for shape in shapes],
        in_specs=[in_smem()] + [pl.BlockSpec(memory_space=pltpu.HBM)] * len(shapes),
        out_specs=[in_vmem()] * len(shapes),
        scratch_shapes=[pltpu.SemaphoreType.DMA((total,))],
        compiler_params=params(),
        cost_estimate=pl.CostEstimate(
            flops=0, bytes_accessed=2 * depth * width, transcendentals=0
        ),
    )(core, *[fixed(value, pltpu.HBM) for value in (*whole, weight)])


def project_kernel(at, a_ref, b_ref, w_ref, v_ref, out_ref):
    for block in range(out_ref.shape[0]):
        total = jnp.dot(a_ref[...], w_ref[at[block]], preferred_element_type=F32)
        total = total + jnp.dot(b_ref[...], v_ref[at[block]], preferred_element_type=F32)
        out_ref[block] = total.astype(out_ref.dtype)


def projected(at, mine, theirs, weight, other_weight, kind):
    count = at.shape[0]
    depth = weight.shape[1]
    return pl.pallas_call(
        project_kernel,
        out_shape=jax.ShapeDtypeStruct((count, ROWS, ROWS), kind),
        in_specs=[in_smem()] + [in_vmem()] * 4,
        out_specs=in_vmem(),
        compiler_params=params(),
        cost_estimate=pl.CostEstimate(
            flops=count * 4 * ROWS * ROWS * depth,
            bytes_accessed=count * 4 * ROWS * depth,
            transcendentals=0,
        ),
    )(at, mine, theirs, fixed(weight), fixed(other_weight))


def shards(
    queries,
    cache_keys,
    cache_values,
    scale_index,
    scale_table,
    hist_lengths,
    span_offsets,
    new_keys,
    new_values,
    head_groups,
    out_weight,
):
    ctx, place = lax.axis_index("ctx"), lax.axis_index("head")
    y, xh = ctx // 2, ctx % 2
    z, xl, core = place // 4, (place // 2) % 2, place % 2

    q0 = jnp.transpose(queries, (1, 0, 2)).reshape(HEADS * ROWS, DH)
    p0 = send(q0, dxh=1, dxl=1)
    q_down = send(q0, dy=1)
    q_up = send(q0, dy=-1)
    pair_groups = send(head_groups, dxh=1, dxl=1)
    lengths = lax.all_to_all(
        jnp.broadcast_to(hist_lengths, (8,)), "ctx", split_axis=0, concat_axis=0, tiled=True
    )
    sent_weight = send(out_weight, dcore=1)
    keys, values, weight = loaded(core[None], out_weight, cache_keys, cache_values)
    start = jnp.sum(jnp.where(jnp.arange(8) < ctx, lengths, 0))
    length = hist_lengths[0]
    p0, q_down, q_up, start, pair_groups, weight = lax.optimization_barrier(
        (p0, q_down, q_up, start, pair_groups, weight)
    )
    q_far = send(q0, dy=2)
    p_down = send(p0, dy=1)
    p_up = send(p0, dy=-1)
    p_far = send(q_far, dxh=1, dxl=1)

    def counts(source_y, source_xh):
        source = (source_y % 4) * 2 + source_xh
        offsets = lax.dynamic_slice_in_dim(span_offsets, source * 2, 2)
        return jnp.clip(jnp.minimum(length, offsets - start), 0, SLOTS)

    def attend(groups, sources, source_xh, queries, previous=None):
        return history(
            groups,
            jnp.concatenate([counts(y + step, source_xh) for step in sources]),
            scale_index,
            scale_table,
            queries,
            keys,
            values,
            previous,
        )

    first = attend(pair_groups, (0,), 1 - xh, [p0])
    back = {0: (send(first, dxh=1, dxl=1), 0)}
    fresh_keys, fresh_values, first = lax.optimization_barrier((new_keys, new_values, first))
    fresh, fresh_lse = fresh_part(
        head_groups,
        q0,
        jnp.transpose(fresh_keys, (1, 0, 2)),
        jnp.transpose(fresh_values, (1, 0, 2)),
    )
    p_down, p_up, p_far, fresh_lse = lax.optimization_barrier((p_down, p_up, p_far, fresh_lse))
    for step, query in ((-1, p_down), (1, p_up), (2, p_far)):
        back[step] = (send(attend(pair_groups, (step,), 1 - xh, [query]), dxh=1, dxl=1), 0)
    parts = []
    for step, query in ((0, q0), (-1, q_down), (1, q_up), (2, q_far)):
        part = attend(head_groups, (step,), xh, [query], back[step])
        parts.append(send(part, dy=step) if step else part)
    sent_weight, _ = lax.optimization_barrier((sent_weight, parts[0]))
    (other_weight,) = loaded(core[None], sent_weight)

    mine = combined(parts, fresh, fresh_lse)
    theirs = send(mine, dcore=1)

    def project(steps, kind, after=None):
        at = jnp.stack([(((z + step) % 8) * 2 + xl) ^ other for step, other in steps])
        if after is not None:
            at, _ = lax.optimization_barrier((at, after))
        return projected(at, mine, theirs, weight, other_weight, kind)

    first = project([(4, 0), (4, 1)], BF16)
    up = send(first[0:1], dz=1)
    down = send(first[1:2], dz=-1)
    whole = project(
        [(step, other) for step in (3, -3, 2, -2, 1, -1, 0) for other in (0, 1)], F32, first
    )
    for step in (3, 2, 1):
        partial = whole[4 * (3 - step) : 4 * (4 - step)]
        if step == 3:
            up = jnp.concatenate([partial[0:1] + up.astype(F32), partial[1:2]])
            down = jnp.concatenate([partial[2:3], partial[3:4] + down.astype(F32)])
        else:
            up = partial[0:2] + up.astype(F32)
            down = partial[2:4] + down.astype(F32)
        up = send(up.astype(BF16), dz=1)
        down = send(down.astype(BF16), dz=-1)
    total = whole[12:14] + up.astype(F32) + down.astype(F32)
    across = send(total[1].astype(BF16), dxl=1)
    return (total[0] + across.astype(F32)).astype(BF16)


def solution(mesh):
    placed = (
        P("ctx", "head", None),
        P(None, "ctx", None),
        P(None, "ctx", None),
        P(None, "ctx"),
        P(),
        P("ctx"),
        P(),
        P("ctx", None, None),
        P("ctx", None, None),
        P("head"),
        P("head", None),
    )
    return jax.shard_map(
        shards, mesh=mesh, in_specs=placed, out_specs=P("ctx", "head"), check_vma=False
    )
```

time: 166 us -> 126 us (0.76)
  Pallas kernels: 59.8 us -> 31 us
  local copies, waits for them, and re-layouts: 17.6 us -> 4.93 us
  waiting for transfers between devices: 31.4 us -> 42.7 us
  starting transfers between devices: 50.5 us -> 42.3 us
  between operations: 4.08 us -> 1.17 us
    pallas_call x9 -> x10, Pallas kernels: 41 us -> 25.3 us  [the longest x8 19.3 us: history(): pl.pallas_call(functools.partial(history_kernel, blocks, at), out_shape=j...]
    ppermute x29 -> x26, starting transfers between devices: 50.5 us -> 36.1 us  [send(): return lax.ppermute(value, AXES, moved(**move))]
    unnamed x27 -> x16, local copies, waits for them, and re-layouts: 17 us -> 3.02 us
    pallas_call x5 -> x2, Pallas kernels: 15.1 us -> 3.58 us  [projected(): pl.pallas_call(project_kernel, out_shape=jax.ShapeDtypeStruct((count, ROW...]
    ppermute x29 -> x26, waiting for transfers between devices: 31.4 us -> 42.7 us  [send(): return lax.ppermute(value, AXES, moved(**move))]
    all_to_all x0 -> x1, starting transfers between devices: none -> 6.18 us  [shards(): lax.all_to_all(jnp.broadcast_to(hist_lengths, (8,)), 'ctx', split_axis=0,...]
  transfers between devices with their start and end apart: 29 -> 27, of which waited for: 10 -> 11; matrix products, arithmetic and copies ran while one was open for 3% -> 3% of each run, Pallas kernels for 29% -> 24%
where the time goes in v2:
time: 126 us; the launch traced here: 125 us
  waiting for transfers between devices  42.7 us (34%)
  starting transfers between devices  42.3 us (34%)
  Pallas kernels  31 us (25%)
  local copies, waits for them, and re-layouts  4.93 us (4%)
  other arithmetic  3.03 us (2%)
    ppermute x26, waiting for transfers between devices, send(): return lax.ppermute(value, AXES, moved(**move))  42.7 us
    ppermute x26, starting transfers between devices, send(): return lax.ppermute(value, AXES, moved(**move))  36.1 us
    pallas_call x8, Pallas kernels, history(): pl.pallas_call(functools.partial(history_kernel, blocks, at), out_shape=j...  19.3 us
    all_to_all x1, starting transfers between devices, shards(): lax.all_to_all(jnp.broadcast_to(hist_lengths, (8,)), 'ctx', split_axis=0,...  6.18 us
    pallas_call x2, Pallas kernels, loaded(): pl.pallas_call(load_kernel, out_shape=[pltpu.VMEM(shape, BF16) for shape...  6.03 us
    pallas_call x2, Pallas kernels, projected(): pl.pallas_call(project_kernel, out_shape=jax.ShapeDtypeStruct((count, ROW...  3.58 us
    unnamed x16, local copies, waits for them, and re-layouts  3.02 us
  transfers between devices with their start and end apart: 27, of which 11 were waited for; matrix products, arithmetic and copies ran while one was open for 3% of the time, Pallas kernels for 24%

profile of v2, /device:TPU:8, one launch (start us, length us, event | category | flops | bytes accessed | tf_op | source)
XLA Modules:
  0.0 125.2 jit_solution(12118929035370932815)
XLA Ops:
  0.0 1.0 copy.18
  1.0 2.3 %collective-permute-start.2 = (bf16[1024,128]{1,0:T(8,128)(2,1)S(1)}, bf16[1024,128]{1,0:T(8,128)(2,1)}, u32[]{:S(2)}, u32[]{:S(2)}) collective-permute-start(bf16[1024,128]{1,0:T(8,128)(2,1)S(1)} %bitcast.34), channel_id=1, source_target_pairs={{0,192},{1,193},{2,194},{3,195},{4,196},{5,197},{6,198},{7,199},{8... | collective-permute-start | bytes 786440 | tf_op jit(solution)/shard_map/ppermute | solution.py:45
  3.3 2.6 %collective-permute-start = (bf16[1024,128]{1,0:T(8,128)(2,1)S(1)}, bf16[1024,128]{1,0:T(8,128)(2,1)}, u32[]{:S(2)}, u32[]{:S(2)}) collective-permute-start(bf16[1024,128]{1,0:T(8,128)(2,1)S(1)} %bitcast.36), channel_id=1, source_target_pairs={{0,34},{1,35},{2,32},{3,33},{4,38},{5,39},{6,36},{7,37},{8,42},{9,... | collective-permute-start | bytes 786440 | tf_op jit(solution)/shard_map/ppermute | solution.py:45
  6.5 0.6 broadcast_in_dim.13
  7.1 6.2 %all-to-all-start = ((s32[8,1,1]{2,1,0:T(1,128)}), s32[8,1,1]{2,1,0:T(1,128)S(1)}, u32[]{:S(2)}, u32[]{:S(2)}) async-start(s32[8,1,1]{2,1,0:T(1,128)} %broadcast_in_dim.13), calls=%async_computation | async-start | bytes 8192 | tf_op jit(solution)/shard_map/all_to_all | solution.py:333
  13.3 2.6 %collective-permute-start.3 = (s32[4]{0:T(128)}, s32[4]{0:T(128)S(1)}, u32[]{:S(2)}, u32[]{:S(2)}) collective-permute-start(s32[4]{0:T(128)} %groups.9), channel_id=1, source_target_pairs={{0,34},{1,35},{2,32},{3,33},{4,38},{5,39},{6,36},{7,37},{8,42},{9,... | collective-permute-start | bytes 56 | tf_op jit(solution)/shard_map/ppermute | solution.py:45
  15.9 3.6 %shard_map.109 = (bf16[8,768,128]{2,1,0:T(8,128)(2,1)S(1)}, bf16[8,768,128]{2,1,0:T(8,128)(2,1)S(1)}, bf16[16,512,256]{2,1,0:T(8,128)(2,1)S(1)}) custom-call(s32[1]{0:T(128)} %bitcast.19.core, bf16[8,768,128]{2,1,0:T(8,128)(2,1)} %refs_0_.1, bf16[8,768,128]{2,1,0:T(8,128)(2,1)} %refs_1_.1, bf16[512,8192]{1,0:T(8,128)(2,1)} %refs_2_.1), custom_call_target="tpu_custom_call" | custom-call | bytes 8388608 | tf_op jit(solution)/shard_map/pallas_call | solution.py:274
  19.5 2.0 %copy-done = bf16[16,512,256]{2,1,0:T(8,128)(2,1)} copy-done((bf16[16,512,256]{2,1,0:T(8,128)(2,1)}, bf16[16,512,256]{2,1,0:T(8,128)(2,1)S(1)}, u32[]{:S(2)}) %copy-start) | copy-done | bytes 4194328
  21.8 2.2 %collective-permute-start.7 = (bf16[1024,128]{1,0:T(8,128)(2,1)S(1)}, bf16[1024,128]{1,0:T(8,128)(2,1)S(1)}, u32[]{:S(2)}, u32[]{:S(2)}) collective-permute-start(bf16[1024,128]{1,0:T(8,128)(2,1)S(1)} %bitcast.37), channel_id=1, source_target_pairs={{0,128},{1,129},{2,130},{3,131},{4,132},{5,133},{6,134},{7,135},{8... | collective-permute-start | bytes 786440 | tf_op jit(solution)/shard_map/ppermute | solution.py:45
  23.9 0.6 fusion.10
  24.6 1.5 %collective-permute-start.6 = (bf16[1024,128]{1,0:T(8,128)(2,1)}, bf16[1024,128]{1,0:T(8,128)(2,1)S(1)}, u32[]{:S(2)}, u32[]{:S(2)}) collective-permute-start(bf16[1024,128]{1,0:T(8,128)(2,1)} %collective-permute-done.refs_0_), channel_id=1, source_target_pairs={{0,192},{1,193},{2,194},{3,195},{4,196},{5,197},{6,198},{7,199},{8... | collective-permute-start | bytes 786440 | tf_op jit(solution)/shard_map/ppermute | solution.py:45
  26.7 0.7 minimum_clamp_fusion
  27.4 2.6 %shard_map.110 = bf16[1,544,256]{2,1,0:T(8,128)(2,1)S(1)} custom-call(s32[4]{0:T(128)S(1)} %collective-permute-done.3.groups, s32[2]{0:T(128)S(1)} %get-tuple-element.56.counts, s32[8,6]{1,0:T(8,128)S(1)} %copy-done.2, f32[2,64]{1,0:T(2,128)S(1)} %copy-done.3, bf16[1024,128]{1,0:T(8,128)(2,1)} %collective-permute-done.refs_0_, ...), custom_call_target="tpu_custom_call" | custom-call | flops 402653184 | bytes 1572864 | tf_op jit(solution)/shard_map/pallas_call | solution.py:162
  30.0 2.6 %collective-permute-done.7.refs_0_ = bf16[1024,128]{1,0:T(8,128)(2,1)S(1)} collective-permute-done((bf16[1024,128]{1,0:T(8,128)(2,1)S(1)}, bf16[1024,128]{1,0:T(8,128)(2,1)S(1)}, u32[]{:S(2)}, u32[]{:S(2)}) %collective-permute-start.7) | collective-permute-done | bytes 262176 | tf_op jit(solution)/shard_map/ppermute | solution.py:45
  33.4 1.8 %shard_map.112 = (f32[512,256]{1,0:T(8,128)S(1)}, f32[8,256]{1,0:T(8,128)S(1)}) custom-call(s32[4]{0:T(128)S(1)} %copy-done.4, bf16[1024,128]{1,0:T(8,128)(2,1)S(1)} %bitcast.38, bf16[8,256,128]{2,1,0:T(8,128)(2,1)S(1)} %get-tuple-element.60.k_ref, bf16[8,256,128]{2,1,0:T(8,128)(2,1)S(1)} %get-tuple-element.59.v_ref), custom_call_target="tpu_custom_call" | custom-call | flops 134217728 | bytes 786432 | tf_op jit(solution)/shard_map/pallas_call | solution.py:202
  35.2 5.0 %collective-permute-done.8.refs_0_ = bf16[1024,128]{1,0:T(8,128)(2,1)S(1)} collective-permute-done((bf16[1024,128]{1,0:T(8,128)(2,1)S(1)}, bf16[1024,128]{1,0:T(8,128)(2,1)S(1)}, u32[]{:S(2)}, u32[]{:S(2)}) %collective-permute-start.8) | collective-permute-done | bytes 262176 | tf_op jit(solution)/shard_map/ppermute | solution.py:45
  40.2 2.3 %shard_map.117 = bf16[1,544,256]{2,1,0:T(8,128)(2,1)S(1)} custom-call(s32[4]{0:T(128)S(1)} %collective-permute-done.3.groups, s32[2]{0:T(128)S(1)} %get-tuple-element.51.counts, s32[8,6]{1,0:T(8,128)S(1)} %copy-done.2, f32[2,64]{1,0:T(2,128)S(1)} %copy-done.3, bf16[1024,128]{1,0:T(8,128)(2,1)S(1)} %collective-permute-done.8.refs_0_, ...), custom_call_target="tpu_custom_call" | custom-call | flops 402653184 | bytes 1572864 | tf_op jit(solution)/shard_map/pallas_call | solution.py:162
  42.5 0.9 collective-permute-start.13
  43.4 2.3 %shard_map.115 = bf16[1,544,256]{2,1,0:T(8,128)(2,1)S(1)} custom-call(s32[4]{0:T(128)S(1)} %collective-permute-done.3.groups, s32[2]{0:T(128)S(1)} %get-tuple-element.52.counts, s32[8,6]{1,0:T(8,128)S(1)} %copy-done.2, f32[2,64]{1,0:T(2,128)S(1)} %copy-done.3, bf16[1024,128]{1,0:T(8,128)(2,1)S(1)} %collective-permute-done.6.refs_0_, ...), custom_call_target="tpu_custom_call" | custom-call | flops 402653184 | bytes 1572864 | tf_op jit(solution)/shard_map/pallas_call | solution.py:162
  45.7 2.7 %collective-permute-start.11 = (bf16[1,544,256]{2,1,0:T(8,128)(2,1)S(1)}, bf16[1,544,256]{2,1,0:T(8,128)(2,1)S(1)}, u32[]{:S(2)}, u32[]{:S(2)}) collective-permute-start(bf16[1,544,256]{2,1,0:T(8,128)(2,1)S(1)} %shard_map.115), channel_id=1, source_target_pairs={{0,34},{1,35},{2,32},{3,33},{4,38},{5,39},{6,36},{7,37},{8,42},{9,... | collective-permute-start | bytes 835592 | tf_op jit(solution)/shard_map/ppermute | solution.py:45
  48.4 2.3 %shard_map.113 = bf16[1,544,256]{2,1,0:T(8,128)(2,1)S(1)} custom-call(s32[4]{0:T(128)S(1)} %collective-permute-done.3.groups, s32[2]{0:T(128)S(1)} %get-tuple-element.54.counts, s32[8,6]{1,0:T(8,128)S(1)} %copy-done.2, f32[2,64]{1,0:T(2,128)S(1)} %copy-done.3, bf16[1024,128]{1,0:T(8,128)(2,1)S(1)} %collective-permute-done.5.refs_0_, ...), custom_call_target="tpu_custom_call" | custom-call | flops 402653184 | bytes 1572864 | tf_op jit(solution)/shard_map/pallas_call | solution.py:162
  50.7 0.7 collective-permute-start.9
  51.3 2.6 %collective-permute-start.4 = (bf16[1,544,256]{2,1,0:T(8,128)(2,1)S(1)}, bf16[1,544,256]{2,1,0:T(8,128)(2,1)S(1)}, u32[]{:S(2)}, u32[]{:S(2)}) collective-permute-start(bf16[1,544,256]{2,1,0:T(8,128)(2,1)S(1)} %shard_map.110), channel_id=1, source_target_pairs={{0,34},{1,35},{2,32},{3,33},{4,38},{5,39},{6,36},{7,37},{8,42},{9,... | collective-permute-start | bytes 835592 | tf_op jit(solution)/shard_map/ppermute | solution.py:45
  54.0 2.3 %shard_map.118 = bf16[1,544,256]{2,1,0:T(8,128)(2,1)S(1)} custom-call(s32[4]{0:T(128)S(1)} %copy-done.4, s32[2]{0:T(128)S(1)} %get-tuple-element.58.counts, s32[8,6]{1,0:T(8,128)S(1)} %copy-done.2, f32[2,64]{1,0:T(2,128)S(1)} %copy-done.3, bf16[1024,128]{1,0:T(8,128)(2,1)S(1)} %collective-permute-done.7.refs_0_, ...), custom_call_target="tpu_custom_call" | custom-call | flops 402653184 | bytes 1572864 | tf_op jit(solution)/shard_map/pallas_call | solution.py:162
  56.3 2.1 %collective-permute-start.14 = (bf16[1,544,256]{2,1,0:T(8,128)(2,1)S(1)}, bf16[1,544,256]{2,1,0:T(8,128)(2,1)S(1)}, u32[]{:S(2)}, u32[]{:S(2)}) collective-permute-start(bf16[1,544,256]{2,1,0:T(8,128)(2,1)S(1)} %shard_map.118), channel_id=1, source_target_pairs={{0,128},{1,129},{2,130},{3,131},{4,132},{5,133},{6,134},{7,135},{8... | collective-permute-start | bytes 835592 | tf_op jit(solution)/shard_map/ppermute | solution.py:45
  58.7 2.6 %shard_map.116 = bf16[1,544,256]{2,1,0:T(8,128)(2,1)S(1)} custom-call(s32[4]{0:T(128)S(1)} %copy-done.4, s32[2]{0:T(128)S(1)} %get-tuple-element.53.counts, s32[8,6]{1,0:T(8,128)S(1)} %copy-done.2, f32[2,64]{1,0:T(2,128)S(1)} %copy-done.3, bf16[1024,128]{1,0:T(8,128)(2,1)} %collective-permute-done.2.refs_0_, ...), custom_call_target="tpu_custom_call" | custom-call | flops 402653184 | bytes 1572864 | tf_op jit(solution)/shard_map/pallas_call | solution.py:162
  61.4 1.2 collective-permute-start.12
  62.6 0.7 collective-permute-done.9.refs_3_
  63.2 2.6 %shard_map.114 = bf16[1,544,256]{2,1,0:T(8,128)(2,1)S(1)} custom-call(s32[4]{0:T(128)S(1)} %copy-done.4, s32[2]{0:T(128)S(1)} %get-tuple-element.55.counts, s32[8,6]{1,0:T(8,128)S(1)} %copy-done.2, f32[2,64]{1,0:T(2,128)S(1)} %copy-done.3, bf16[1024,128]{1,0:T(8,128)(2,1)} %collective-permute-done.1.refs_0_, ...), custom_call_target="tpu_custom_call" | custom-call | flops 402653184 | bytes 1572864 | tf_op jit(solution)/shard_map/pallas_call | solution.py:162
  65.9 0.6 collective-permute-start.10
  66.5 2.3 %shard_map.111.a_ref = bf16[1,544,256]{2,1,0:T(8,128)(2,1)S(1)} custom-call(s32[4]{0:T(128)S(1)} %copy-done.4, s32[2]{0:T(128)S(1)} %get-tuple-element.57.counts, s32[8,6]{1,0:T(8,128)S(1)} %copy-done.2, f32[2,64]{1,0:T(2,128)S(1)} %copy-done.3, bf16[1024,128]{1,0:T(8,128)(2,1)S(1)} %bitcast.39, bf16[8,768,128]{2,1,0:T(8,128)(2,1)S(1)} %get-tuple-element.26.refs_1_, ...), custom_call_target="tpu_custom_call" | custom-call | flops 402653184 | bytes 1572864 | tf_op jit(solution)/shard_map/pallas_call | solution.py:162
  68.8 3.9 %collective-permute-done.10.b_ref = bf16[1,544,256]{2,1,0:T(8,128)(2,1)S(1)} collective-permute-done((bf16[1,544,256]{2,1,0:T(8,128)(2,1)S(1)}, bf16[1,544,256]{2,1,0:T(8,128)(2,1)S(1)}, u32[]{:S(2)}, u32[]{:S(2)}) %collective-permute-start.10) | collective-permute-done | bytes 278560 | tf_op jit(solution)/shard_map/ppermute | solution.py:45
  73.5 2.5 %shard_map.120.v_ref = bf16[16,512,256]{2,1,0:T(8,128)(2,1)S(1)} custom-call(s32[1]{0:T(128)} %bitcast.19.core, bf16[512,8192]{1,0:T(8,128)(2,1)} %collective-permute-done.16.refs_0_), custom_call_target="tpu_custom_call" | custom-call | bytes 8388608 | tf_op jit(solution)/shard_map/pallas_call | solution.py:274
  76.0 1.0 copy-done.1
  77.0 1.0 shard_map.121
  78.0 2.0 %collective-permute-start.17 = (bf16[1,256,256]{2,1,0:T(8,128)(2,1)S(1)}, bf16[1,256,256]{2,1,0:T(8,128)(2,1)S(1)}, u32[]{:S(2)}, u32[]{:S(2)}) collective-permute-start(bf16[1,256,256]{2,1,0:T(8,128)(2,1)S(1)} %get-tuple-element.49), channel_id=1, source_target_pairs={{0,4},{1,5},{2,6},{3,7},{4,8},{5,9},{6,10},{7,11},{8,12},{9,13},{1... | collective-permute-start | bytes 393224 | tf_op jit(solution)/shard_map/ppermute | solution.py:45
  80.0 4.0 %collective-permute-start.21 = (bf16[1,256,256]{2,1,0:T(8,128)(2,1)S(1)}, bf16[1,256,256]{2,1,0:T(8,128)(2,1)S(1)}, u32[]{:S(2)}, u32[]{:S(2)}) collective-permute-start(bf16[1,256,256]{2,1,0:T(8,128)(2,1)S(1)} %get-tuple-element.50), channel_id=1, source_target_pairs={{0,28},{1,29},{2,30},{3,31},{4,0},{5,1},{6,2},{7,3},{8,4},{9,5},{1... | collective-permute-start | bytes 393224 | tf_op jit(solution)/shard_map/ppermute | solution.py:45
  84.1 2.6 %shard_map.122 = f32[14,256,256]{2,1,0:T(8,128)S(1)} custom-call(s32[14]{0:T(128)S(1)} %stack.68.at, bf16[256,512]{1,0:T(8,128)(2,1)S(1)} %shard_map.119.a_ref, bf16[256,512]{1,0:T(8,128)(2,1)S(1)} %collective-permute-done.15.b_ref, bf16[16,512,256]{2,1,0:T(8,128)(2,1)S(1)} %copy-done.1, bf16[16,512,256]{2,1,0:T(8,128)(2,1)S(1)} %shard_map.120.v_ref), custom_call_target="tpu_custom_call" | custom-call | flops 1879048192 | bytes 7340032 | tf_op jit(solution)/shard_map/pallas_call | solution.py:297
  86.9 1.0 collective-permute-done.17
  88.2 3.3 %collective-permute-start.22 = (bf16[2,256,256]{2,1,0:T(8,128)(2,1)S(1)}, bf16[2,256,256]{2,1,0:T(8,128)(2,1)S(1)}, u32[]{:S(2)}, u32[]{:S(2)}) collective-permute-start(bf16[2,256,256]{2,1,0:T(8,128)(2,1)S(1)} %pad_maximum_fusion.1), channel_id=1, source_target_pairs={{0,28},{1,29},{2,30},{3,31},{4,0},{5,1},{6,2},{7,3},{8,4},{9,5},{1... | collective-permute-start | bytes 786440 | tf_op jit(solution)/shard_map/ppermute | solution.py:45
  91.5 5.9 %collective-permute-done.18 = bf16[2,256,256]{2,1,0:T(8,128)(2,1)S(1)} collective-permute-done((bf16[2,256,256]{2,1,0:T(8,128)(2,1)S(1)}, bf16[2,256,256]{2,1,0:T(8,128)(2,1)S(1)}, u32[]{:S(2)}, u32[]{:S(2)}) %collective-permute-start.18) | collective-permute-done | bytes 262176 | tf_op jit(solution)/shard_map/ppermute | solution.py:45
  97.6 8.3 %collective-permute-done.19 = bf16[2,256,256]{2,1,0:T(8,128)(2,1)S(1)} collective-permute-done((bf16[2,256,256]{2,1,0:T(8,128)(2,1)S(1)}, bf16[2,256,256]{2,1,0:T(8,128)(2,1)S(1)}, u32[]{:S(2)}, u32[]{:S(2)}) %collective-permute-start.19) | collective-permute-done | bytes 262176 | tf_op jit(solution)/shard_map/ppermute | solution.py:45
  106.1 2.0 %collective-permute-start.20 = (bf16[2,256,256]{2,1,0:T(8,128)(2,1)S(1)}, bf16[2,256,256]{2,1,0:T(8,128)(2,1)S(1)}, u32[]{:S(2)}, u32[]{:S(2)}) collective-permute-start(bf16[2,256,256]{2,1,0:T(8,128)(2,1)S(1)} %get-tuple-element.43), channel_id=1, source_target_pairs={{0,4},{1,5},{2,6},{3,7},{4,8},{5,9},{6,10},{7,11},{8,12},{9,13},{1... | collective-permute-start | bytes 786440 | tf_op jit(solution)/shard_map/ppermute | solution.py:45
  108.2 4.7 %collective-permute-done.23 = bf16[2,256,256]{2,1,0:T(8,128)(2,1)S(1)} collective-permute-done((bf16[2,256,256]{2,1,0:T(8,128)(2,1)S(1)}, bf16[2,256,256]{2,1,0:T(8,128)(2,1)S(1)}, u32[]{:S(2)}, u32[]{:S(2)}) %collective-permute-start.23) | collective-permute-done | bytes 262176 | tf_op jit(solution)/shard_map/ppermute | solution.py:45
  112.9 1.1 collective-permute-start.24
  114.0 5.3 %collective-permute-done.24 = bf16[2,256,256]{2,1,0:T(8,128)(2,1)S(1)} collective-permute-done((bf16[2,256,256]{2,1,0:T(8,128)(2,1)S(1)}, bf16[2,256,256]{2,1,0:T(8,128)(2,1)S(1)}, u32[]{:S(2)}, u32[]{:S(2)}) %collective-permute-start.24) | collective-permute-done | bytes 262176 | tf_op jit(solution)/shard_map/ppermute | solution.py:45
  119.5 5.0 %collective-permute-done.25 = bf16[256,256]{1,0:T(8,128)(2,1)S(1)} collective-permute-done((bf16[256,256]{1,0:T(8,128)(2,1)S(1)}, bf16[256,256]{1,0:T(8,128)(2,1)S(1)}, u32[]{:S(2)}, u32[]{:S(2)}) %collective-permute-start.25) | collective-permute-done | bytes 131104 | tf_op jit(solution)/shard_map/ppermute | solution.py:45
  124.5 0.7 fusion.6
  (56 shorter events, 3.6 us)
Async XLA Ops:
  0.0 73.5 %collective-permute-start.16 = (bf16[512,8192]{1,0:T(8,128)(2,1)}, bf16[512,8192]{1,0:T(8,128)(2,1)}, u32[]{:S(2)}, u32[]{:S(2)}) collective-permute-start(bf16[512,8192]{1,0:T(8,128)(2,1)} %refs_2_.1), channel_id=1, source_target_pairs={{0,1},{1,0},{2,3},{3,2},{4,5},{5,4},{6,7},{7,6},{8,9},{9,8},{10,11... | collective-permute-start | bytes 25165832 | tf_op jit(solution)/shard_map/ppermute | solution.py:45
  1.0 23.6 %collective-permute-start.2 = (bf16[1024,128]{1,0:T(8,128)(2,1)S(1)}, bf16[1024,128]{1,0:T(8,128)(2,1)}, u32[]{:S(2)}, u32[]{:S(2)}) collective-permute-start(bf16[1024,128]{1,0:T(8,128)(2,1)S(1)} %bitcast.34), channel_id=1, source_target_pairs={{0,192},{1,193},{2,194},{3,195},{4,196},{5,197},{6,198},{7,199},{8... | collective-permute-start | bytes 786440 | tf_op jit(solution)/shard_map/ppermute | solution.py:45
  3.3 21.3 %collective-permute-start.1 = (bf16[1024,128]{1,0:T(8,128)(2,1)S(1)}, bf16[1024,128]{1,0:T(8,128)(2,1)}, u32[]{:S(2)}, u32[]{:S(2)}) collective-permute-start(bf16[1024,128]{1,0:T(8,128)(2,1)S(1)} %bitcast.35), channel_id=1, source_target_pairs={{0,64},{1,65},{2,66},{3,67},{4,68},{5,69},{6,70},{7,71},{8,72},{9,... | collective-permute-start | bytes 786440 | tf_op jit(solution)/shard_map/ppermute | solution.py:45
  3.3 21.3 %collective-permute-start = (bf16[1024,128]{1,0:T(8,128)(2,1)S(1)}, bf16[1024,128]{1,0:T(8,128)(2,1)}, u32[]{:S(2)}, u32[]{:S(2)}) collective-permute-start(bf16[1024,128]{1,0:T(8,128)(2,1)S(1)} %bitcast.36), channel_id=1, source_target_pairs={{0,34},{1,35},{2,32},{3,33},{4,38},{5,39},{6,36},{7,37},{8,42},{9,... | collective-permute-start | bytes 786440 | tf_op jit(solution)/shard_map/ppermute | solution.py:45
  7.1 14.4 %all-to-all-start = ((s32[8,1,1]{2,1,0:T(1,128)}), s32[8,1,1]{2,1,0:T(1,128)S(1)}, u32[]{:S(2)}, u32[]{:S(2)}) async-start(s32[8,1,1]{2,1,0:T(1,128)} %broadcast_in_dim.13), calls=%async_computation | async-start | bytes 8192 | tf_op jit(solution)/shard_map/all_to_all | solution.py:333
  13.3 8.5 %collective-permute-start.3 = (s32[4]{0:T(128)}, s32[4]{0:T(128)S(1)}, u32[]{:S(2)}, u32[]{:S(2)}) collective-permute-start(s32[4]{0:T(128)} %groups.9), channel_id=1, source_target_pairs={{0,34},{1,35},{2,32},{3,33},{4,38},{5,39},{6,36},{7,37},{8,42},{9,... | collective-permute-start | bytes 56 | tf_op jit(solution)/shard_map/ppermute | solution.py:45
  15.9 10.7 %copy-start.7 = (s32[16]{0:T(128)S(1)}, s32[16]{0:T(128)}, u32[]{:S(2)}) copy-start(s32[16]{0:T(128)} %param.17) | copy-start | bytes 196
  15.9 11.5 %copy-start.2 = (s32[8,6]{1,0:T(8,128)S(1)}, s32[8,6]{1,0:T(8,128)}, u32[]{:S(2)}) copy-start(s32[8,6]{1,0:T(8,128)} %scale_index.15) | copy-start | bytes 580
  15.9 11.5 %copy-start.3 = (f32[2,64]{1,0:T(2,128)S(1)}, f32[2,64]{1,0:T(2,128)}, u32[]{:S(2)}) copy-start(f32[2,64]{1,0:T(2,128)} %scale_table.15) | copy-start | bytes 1540
  19.5 2.0 %copy-start = (bf16[16,512,256]{2,1,0:T(8,128)(2,1)}, bf16[16,512,256]{2,1,0:T(8,128)(2,1)S(1)}, u32[]{:S(2)}) copy-start(bf16[16,512,256]{2,1,0:T(8,128)(2,1)S(1)} %get-tuple-element.40.w_ref) | copy-start | bytes 12582916
  21.5 11.9 %copy-start.4 = (s32[4]{0:T(128)S(1)}, s32[4]{0:T(128)}, u32[]{:S(2)}) copy-start(s32[4]{0:T(128)} %groups.9) | copy-start | bytes 52
  21.7 11.5 %copy-start.5 = (bf16[256,8,128]{2,1,0:T(8,128)(2,1)S(1)}, bf16[256,8,128]{2,1,0:T(8,128)(2,1)}, u32[]{:S(2)}) copy-start(bf16[256,8,128]{2,1,0:T(8,128)(2,1)} %param.19) | copy-start | bytes 1572868
  21.7 11.5 %copy-start.6 = (bf16[256,8,128]{2,1,0:T(8,128)(2,1)S(1)}, bf16[256,8,128]{2,1,0:T(8,128)(2,1)}, u32[]{:S(2)}) copy-start(bf16[256,8,128]{2,1,0:T(8,128)(2,1)} %param.18) | copy-start | bytes 1572868
  21.8 10.9 %collective-permute-start.7 = (bf16[1024,128]{1,0:T(8,128)(2,1)S(1)}, bf16[1024,128]{1,0:T(8,128)(2,1)S(1)}, u32[]{:S(2)}, u32[]{:S(2)}) collective-permute-start(bf16[1024,128]{1,0:T(8,128)(2,1)S(1)} %bitcast.37), channel_id=1, source_target_pairs={{0,128},{1,129},{2,130},{3,131},{4,132},{5,133},{6,134},{7,135},{8... | collective-permute-start | bytes 786440 | tf_op jit(solution)/shard_map/ppermute | solution.py:45
  24.6 15.7 %collective-permute-start.6 = (bf16[1024,128]{1,0:T(8,128)(2,1)}, bf16[1024,128]{1,0:T(8,128)(2,1)S(1)}, u32[]{:S(2)}, u32[]{:S(2)}) collective-permute-start(bf16[1024,128]{1,0:T(8,128)(2,1)} %collective-permute-done.refs_0_), channel_id=1, source_target_pairs={{0,192},{1,193},{2,194},{3,195},{4,196},{5,197},{6,198},{7,199},{8... | collective-permute-start | bytes 786440 | tf_op jit(solution)/shard_map/ppermute | solution.py:45
  26.1 14.1 %collective-permute-start.5 = (bf16[1024,128]{1,0:T(8,128)(2,1)}, bf16[1024,128]{1,0:T(8,128)(2,1)S(1)}, u32[]{:S(2)}, u32[]{:S(2)}) collective-permute-start(bf16[1024,128]{1,0:T(8,128)(2,1)} %collective-permute-done.refs_0_), channel_id=1, source_target_pairs={{0,64},{1,65},{2,66},{3,67},{4,68},{5,69},{6,70},{7,71},{8,72},{9,... | collective-permute-start | bytes 786440 | tf_op jit(solution)/shard_map/ppermute | solution.py:45
  32.6 7.6 %collective-permute-start.8 = (bf16[1024,128]{1,0:T(8,128)(2,1)S(1)}, bf16[1024,128]{1,0:T(8,128)(2,1)S(1)}, u32[]{:S(2)}, u32[]{:S(2)}) collective-permute-start(bf16[1024,128]{1,0:T(8,128)(2,1)S(1)} %collective-permute-done.7.refs_0_), channel_id=1, source_target_pairs={{0,34},{1,35},{2,32},{3,33},{4,38},{5,39},{6,36},{7,37},{8,42},{9,... | collective-permute-start | bytes 786440 | tf_op jit(solution)/shard_map/ppermute | solution.py:45
  42.5 11.5 %collective-permute-start.13 = (bf16[1,544,256]{2,1,0:T(8,128)(2,1)S(1)}, bf16[1,544,256]{2,1,0:T(8,128)(2,1)S(1)}, u32[]{:S(2)}, u32[]{:S(2)}) collective-permute-start(bf16[1,544,256]{2,1,0:T(8,128)(2,1)S(1)} %shard_map.117), channel_id=1, source_target_pairs={{0,34},{1,35},{2,32},{3,33},{4,38},{5,39},{6,36},{7,37},{8,42},{9,... | collective-permute-start | bytes 835592 | tf_op jit(solution)/shard_map/ppermute | solution.py:45
  45.7 13.1 %collective-permute-start.11 = (bf16[1,544,256]{2,1,0:T(8,128)(2,1)S(1)}, bf16[1,544,256]{2,1,0:T(8,128)(2,1)S(1)}, u32[]{:S(2)}, u32[]{:S(2)}) collective-permute-start(bf16[1,544,256]{2,1,0:T(8,128)(2,1)S(1)} %shard_map.115), channel_id=1, source_target_pairs={{0,34},{1,35},{2,32},{3,33},{4,38},{5,39},{6,36},{7,37},{8,42},{9,... | collective-permute-start | bytes 835592 | tf_op jit(solution)/shard_map/ppermute | solution.py:45
  50.7 12.6 %collective-permute-start.9 = (bf16[1,544,256]{2,1,0:T(8,128)(2,1)S(1)}, bf16[1,544,256]{2,1,0:T(8,128)(2,1)S(1)}, u32[]{:S(2)}, u32[]{:S(2)}) collective-permute-start(bf16[1,544,256]{2,1,0:T(8,128)(2,1)S(1)} %shard_map.113), channel_id=1, source_target_pairs={{0,34},{1,35},{2,32},{3,33},{4,38},{5,39},{6,36},{7,37},{8,42},{9,... | collective-permute-start | bytes 835592 | tf_op jit(solution)/shard_map/ppermute | solution.py:45
  51.3 15.2 %collective-permute-start.4 = (bf16[1,544,256]{2,1,0:T(8,128)(2,1)S(1)}, bf16[1,544,256]{2,1,0:T(8,128)(2,1)S(1)}, u32[]{:S(2)}, u32[]{:S(2)}) collective-permute-start(bf16[1,544,256]{2,1,0:T(8,128)(2,1)S(1)} %shard_map.110), channel_id=1, source_target_pairs={{0,34},{1,35},{2,32},{3,33},{4,38},{5,39},{6,36},{7,37},{8,42},{9,... | collective-permute-start | bytes 835592 | tf_op jit(solution)/shard_map/ppermute | solution.py:45
  56.3 12.5 %collective-permute-start.14 = (bf16[1,544,256]{2,1,0:T(8,128)(2,1)S(1)}, bf16[1,544,256]{2,1,0:T(8,128)(2,1)S(1)}, u32[]{:S(2)}, u32[]{:S(2)}) collective-permute-start(bf16[1,544,256]{2,1,0:T(8,128)(2,1)S(1)} %shard_map.118), channel_id=1, source_target_pairs={{0,128},{1,129},{2,130},{3,131},{4,132},{5,133},{6,134},{7,135},{8... | collective-permute-start | bytes 835592 | tf_op jit(solution)/shard_map/ppermute | solution.py:45
  61.4 7.5 %collective-permute-start.12 = (bf16[1,544,256]{2,1,0:T(8,128)(2,1)S(1)}, bf16[1,544,256]{2,1,0:T(8,128)(2,1)S(1)}, u32[]{:S(2)}, u32[]{:S(2)}) collective-permute-start(bf16[1,544,256]{2,1,0:T(8,128)(2,1)S(1)} %shard_map.116), channel_id=1, source_target_pairs={{0,64},{1,65},{2,66},{3,67},{4,68},{5,69},{6,70},{7,71},{8,72},{9,... | collective-permute-start | bytes 835592 | tf_op jit(solution)/shard_map/ppermute | solution.py:45
  65.9 6.8 %collective-permute-start.10 = (bf16[1,544,256]{2,1,0:T(8,128)(2,1)S(1)}, bf16[1,544,256]{2,1,0:T(8,128)(2,1)S(1)}, u32[]{:S(2)}, u32[]{:S(2)}) collective-permute-start(bf16[1,544,256]{2,1,0:T(8,128)(2,1)S(1)} %shard_map.114), channel_id=1, source_target_pairs={{0,192},{1,193},{2,194},{3,195},{4,196},{5,197},{6,198},{7,199},{8... | collective-permute-start | bytes 835592 | tf_op jit(solution)/shard_map/ppermute | solution.py:45
  73.1 2.9 %collective-permute-start.15 = (bf16[256,512]{1,0:T(8,128)(2,1)S(1)}, bf16[256,512]{1,0:T(8,128)(2,1)S(1)}, u32[]{:S(2)}, u32[]{:S(2)}) collective-permute-start(bf16[256,512]{1,0:T(8,128)(2,1)S(1)} %shard_map.119.a_ref), channel_id=1, source_target_pairs={{0,1},{1,0},{2,3},{3,2},{4,5},{5,4},{6,7},{7,6},{8,9},{9,8},{10,11... | collective-permute-start | bytes 786440 | tf_op jit(solution)/shard_map/ppermute | solution.py:45
  73.5 3.5 %copy-start.1 = (bf16[16,512,256]{2,1,0:T(8,128)(2,1)S(1)}, bf16[16,512,256]{2,1,0:T(8,128)(2,1)}, u32[]{:S(2)}) copy-start(bf16[16,512,256]{2,1,0:T(8,128)(2,1)} %copy-done) | copy-start | bytes 12582916
  78.0 9.9 %collective-permute-start.17 = (bf16[1,256,256]{2,1,0:T(8,128)(2,1)S(1)}, bf16[1,256,256]{2,1,0:T(8,128)(2,1)S(1)}, u32[]{:S(2)}, u32[]{:S(2)}) collective-permute-start(bf16[1,256,256]{2,1,0:T(8,128)(2,1)S(1)} %get-tuple-element.49), channel_id=1, source_target_pairs={{0,4},{1,5},{2,6},{3,7},{4,8},{5,9},{6,10},{7,11},{8,12},{9,13},{1... | collective-permute-start | bytes 393224 | tf_op jit(solution)/shard_map/ppermute | solution.py:45
  80.0 7.9 %collective-permute-start.21 = (bf16[1,256,256]{2,1,0:T(8,128)(2,1)S(1)}, bf16[1,256,256]{2,1,0:T(8,128)(2,1)S(1)}, u32[]{:S(2)}, u32[]{:S(2)}) collective-permute-start(bf16[1,256,256]{2,1,0:T(8,128)(2,1)S(1)} %get-tuple-element.50), channel_id=1, source_target_pairs={{0,28},{1,29},{2,30},{3,31},{4,0},{5,1},{6,2},{7,3},{8,4},{9,5},{1... | collective-permute-start | bytes 393224 | tf_op jit(solution)/shard_map/ppermute | solution.py:45
  88.1 9.3 %collective-permute-start.18 = (bf16[2,256,256]{2,1,0:T(8,128)(2,1)S(1)}, bf16[2,256,256]{2,1,0:T(8,128)(2,1)S(1)}, u32[]{:S(2)}, u32[]{:S(2)}) collective-permute-start(bf16[2,256,256]{2,1,0:T(8,128)(2,1)S(1)} %pad_maximum_fusion), channel_id=1, source_target_pairs={{0,4},{1,5},{2,6},{3,7},{4,8},{5,9},{6,10},{7,11},{8,12},{9,13},{1... | collective-permute-start | bytes 786440 | tf_op jit(solution)/shard_map/ppermute | solution.py:45
  88.2 9.4 %collective-permute-start.22 = (bf16[2,256,256]{2,1,0:T(8,128)(2,1)S(1)}, bf16[2,256,256]{2,1,0:T(8,128)(2,1)S(1)}, u32[]{:S(2)}, u32[]{:S(2)}) collective-permute-start(bf16[2,256,256]{2,1,0:T(8,128)(2,1)S(1)} %pad_maximum_fusion.1), channel_id=1, source_target_pairs={{0,28},{1,29},{2,30},{3,31},{4,0},{5,1},{6,2},{7,3},{8,4},{9,5},{1... | collective-permute-start | bytes 786440 | tf_op jit(solution)/shard_map/ppermute | solution.py:45
  97.5 8.5 %collective-permute-start.19 = (bf16[2,256,256]{2,1,0:T(8,128)(2,1)S(1)}, bf16[2,256,256]{2,1,0:T(8,128)(2,1)S(1)}, u32[]{:S(2)}, u32[]{:S(2)}) collective-permute-start(bf16[2,256,256]{2,1,0:T(8,128)(2,1)S(1)} %fusion.2), channel_id=1, source_target_pairs={{0,4},{1,5},{2,6},{3,7},{4,8},{5,9},{6,10},{7,11},{8,12},{9,13},{1... | collective-permute-start | bytes 786440 | tf_op jit(solution)/shard_map/ppermute | solution.py:45
  106.0 6.8 %collective-permute-start.23 = (bf16[2,256,256]{2,1,0:T(8,128)(2,1)S(1)}, bf16[2,256,256]{2,1,0:T(8,128)(2,1)S(1)}, u32[]{:S(2)}, u32[]{:S(2)}) collective-permute-start(bf16[2,256,256]{2,1,0:T(8,128)(2,1)S(1)} %get-tuple-element.44), channel_id=1, source_target_pairs={{0,28},{1,29},{2,30},{3,31},{4,0},{5,1},{6,2},{7,3},{8,4},{9,5},{1... | collective-permute-start | bytes 786440 | tf_op jit(solution)/shard_map/ppermute | solution.py:45
  106.1 7.9 %collective-permute-start.20 = (bf16[2,256,256]{2,1,0:T(8,128)(2,1)S(1)}, bf16[2,256,256]{2,1,0:T(8,128)(2,1)S(1)}, u32[]{:S(2)}, u32[]{:S(2)}) collective-permute-start(bf16[2,256,256]{2,1,0:T(8,128)(2,1)S(1)} %get-tuple-element.43), channel_id=1, source_target_pairs={{0,4},{1,5},{2,6},{3,7},{4,8},{5,9},{6,10},{7,11},{8,12},{9,13},{1... | collective-permute-start | bytes 786440 | tf_op jit(solution)/shard_map/ppermute | solution.py:45
  112.9 6.5 %collective-permute-start.24 = (bf16[2,256,256]{2,1,0:T(8,128)(2,1)S(1)}, bf16[2,256,256]{2,1,0:T(8,128)(2,1)S(1)}, u32[]{:S(2)}, u32[]{:S(2)}) collective-permute-start(bf16[2,256,256]{2,1,0:T(8,128)(2,1)S(1)} %fusion.1), channel_id=1, source_target_pairs={{0,28},{1,29},{2,30},{3,31},{4,0},{5,1},{6,2},{7,3},{8,4},{9,5},{1... | collective-permute-start | bytes 786440 | tf_op jit(solution)/shard_map/ppermute | solution.py:45
  119.4 5.1 %collective-permute-start.25 = (bf16[256,256]{1,0:T(8,128)(2,1)S(1)}, bf16[256,256]{1,0:T(8,128)(2,1)S(1)}, u32[]{:S(2)}, u32[]{:S(2)}) collective-permute-start(bf16[256,256]{1,0:T(8,128)(2,1)S(1)} %fusion.9), channel_id=1, source_target_pairs={{0,2},{1,3},{2,0},{3,1},{4,6},{5,7},{6,4},{7,5},{8,10},{9,11},{10,... | collective-permute-start | bytes 393224 | tf_op jit(solution)/shard_map/ppermute | solution.py:45
